TPU v7x, 512 devices: a whole 4x4x16 slice. The times are simulated.
512 devices in a mesh: seq: 64 (over x, z_hi, y), tp: 8 (over z_lo, core).
Axes of the slice: x: 4, y: 4, z: 16 (z_hi: 4, z_lo: 4; z = z_hi * 4 + z_lo), core: 2. Of those that a mesh axis runs over, the one named last changes fastest.
Arguments:
- signal: bfloat16 [8192, 4096], P('seq', 'tp'), may hold values from -6 to 6
- gate_input: bfloat16 [8192, 4096], P('seq', 'tp'), may hold values from -6 to 6
- filters: bfloat16 [1024, 4096], P(None, 'tp'), may hold values from -0.1875 to 0.1875
- skip_weight: float32 [4096], P('tp'), may hold values from 0.2 to 5, as said below
- doc_lengths: int32 [16], replicated, may hold values from 1 to 8, 64 in all
- grad_out: bfloat16 [8192, 4096], P('seq', 'tp'), may hold values from -6 to 6
Outputs:
- output: bfloat16 [8192, 4096], P('seq', 'tp')
- grad_signal: bfloat16 [8192, 4096], P('seq', 'tp')
- grad_gate: bfloat16 [8192, 4096], P('seq', 'tp')
- grad_filters: float32 [1024, 4096], P('seq', 'tp')
Inputs may be any that keep to these rules, and one draw needn't show every extreme that they name: `doc_lengths`: lengths of the 16 packed documents in blocks of 128 tokens; they sum to 64 and the largest is exactly 8. `skip_weight`: positive per-channel weights.
All inputs are finite; a program needn't handle non-finite values.
Results may differ from a plain program's by a relative error of at most 0.0049.
Values may be sent and summed in bfloat16 or wider, within the bound.
A program may use at most 64 MiB of HBM per device.

v0:
```python
import math

import jax
import jax.numpy as jnp
from jax import lax
from jax.sharding import PartitionSpec as P

EPSILON = 1e-06
HIGHEST = lax.Precision.HIGHEST


def from_behind(value, axis, steps):
    count = lax.axis_size(axis)
    initial, last = (max(0, -steps), min(count, count - steps))
    return lax.ppermute(value, axis, [(source, source + steps) for source in range(initial, last)])


def tables(block_rows):
    period = 2 * block_rows
    freq_grid = lax.broadcasted_iota(jnp.int32, (period, period), 0)
    time_grid = lax.broadcasted_iota(jnp.int32, (period, period), 1)
    phase = (freq_grid * time_grid % period).astype(jnp.float32) * (2.0 * math.pi / period)
    return (jnp.cos(phase), jnp.sin(phase))


def product(matrix, values):
    return jnp.dot(matrix, values, precision=HIGHEST, preferred_element_type=jnp.float32)


def spectrum(cos_table, sin_table, values, offset):
    amount = values.shape[0]
    cos_part = lax.slice_in_dim(cos_table, offset, offset + amount, axis=1)
    sin_part = lax.slice_in_dim(sin_table, offset, offset + amount, axis=1)
    return (product(cos_part, values), -product(sin_part, values))


def inverse(cos_table, sin_table, real_part, imag_part, offset, amount):
    period = cos_table.shape[0]
    cos_part = lax.slice_in_dim(cos_table, offset, offset + amount, axis=0)
    sin_part = lax.slice_in_dim(sin_table, offset, offset + amount, axis=0)
    return (product(cos_part, real_part) - product(sin_part, imag_part)) / period


def doc_bounds(doc_lengths, position):
    finish = jnp.cumsum(doc_lengths)
    anchor = finish - doc_lengths
    inside = (anchor <= position) & (position < finish)
    first_block = jnp.sum(jnp.where(inside, anchor, 0))
    end_block = jnp.sum(jnp.where(inside, finish, 0))
    return (first_block, end_block)


def on_device(signal, gate_input, filters, skip_weight, doc_lengths, grad_out):
    block_rows, channels = signal.shape
    period = 2 * block_rows
    lag_blocks = filters.shape[0] // block_rows
    cos_table, sin_table = tables(block_rows)
    alternate = (1 - 2 * (lax.broadcasted_iota(jnp.int32, (period, 1), 0) % 2)).astype(jnp.float32)
    position = lax.axis_index("seq")
    first_block, end_block = doc_bounds(doc_lengths, position)
    tap_values = filters.astype(jnp.float32)
    pieces = [
        spectrum(
            cos_table, sin_table, tap_values[number * block_rows : (number + 1) * block_rows], 0
        )
        for number in range(lag_blocks)
    ]
    kernels = []
    for distance in range(lag_blocks):
        kernel_real = alternate * pieces[distance][0]
        kernel_imag = alternate * pieces[distance][1]
        if distance > 0:
            kernel_real = kernel_real + pieces[distance - 1][0]
            kernel_imag = kernel_imag + pieces[distance - 1][1]
        kernels.append((kernel_real, kernel_imag))
    signal_f = signal.astype(jnp.float32)
    own_spec = spectrum(cos_table, sin_table, signal_f, 0)
    sources = [own_spec]
    for distance in range(1, lag_blocks):
        earlier = from_behind(signal, "seq", distance)
        sources.append(spectrum(cos_table, sin_table, earlier.astype(jnp.float32), 0))
    live_early = [
        (position - distance >= first_block).astype(jnp.float32) for distance in range(lag_blocks)
    ]
    conv_real = jnp.zeros((period, channels), jnp.float32)
    conv_imag = jnp.zeros((period, channels), jnp.float32)
    for distance in range(lag_blocks):
        kernel_real, kernel_imag = kernels[distance]
        source_real, source_imag = sources[distance]
        conv_real = conv_real + live_early[distance] * (
            kernel_real * source_real - kernel_imag * source_imag
        )
        conv_imag = conv_imag + live_early[distance] * (
            kernel_real * source_imag + kernel_imag * source_real
        )
    convolved = inverse(cos_table, sin_table, conv_real, conv_imag, block_rows, block_rows)
    mixed = convolved + skip_weight[None, :] * signal_f
    gate_f = gate_input.astype(jnp.float32)
    gated = gate_f * mixed
    cotangent = grad_out.astype(jnp.float32)
    total_channels = channels * lax.axis_size("tp")
    squares = jnp.sum(gated * gated, axis=1)
    squares = lax.psum(squares, "tp")
    inverse_rms = lax.rsqrt(squares / total_channels + EPSILON)[:, None]
    output = (gated * inverse_rms).astype(jnp.bfloat16)
    projection = lax.psum(jnp.sum(cotangent * gated, axis=1), "tp")
    mean_proj = (projection / total_channels)[:, None]
    grad_gated = cotangent * inverse_rms - gated * (
        mean_proj * inverse_rms * inverse_rms * inverse_rms
    )
    grad_gate = (grad_gated * mixed).astype(jnp.bfloat16)
    grad_mixed16 = (grad_gated * gate_f).astype(jnp.bfloat16)
    grad_mixed = lax.optimization_barrier(grad_mixed16).astype(jnp.float32)
    dz_real, dz_imag = spectrum(cos_table, sin_table, grad_mixed, block_rows)
    kernel_real, kernel_imag = kernels[0]
    back_real = kernel_real * dz_real + kernel_imag * dz_imag
    back_imag = kernel_real * dz_imag - kernel_imag * dz_real
    accum = (back_real, back_imag)
    for distance in range(1, lag_blocks):
        later = from_behind(grad_mixed16, "seq", -distance)
        live = (position + distance < end_block).astype(jnp.float32)
        later_real, later_imag = spectrum(
            cos_table, sin_table, later.astype(jnp.float32), block_rows
        )
        kern_real, kern_imag = kernels[distance]
        accum = (
            accum[0] + live * (kern_real * later_real + kern_imag * later_imag),
            accum[1] + live * (kern_real * later_imag - kern_imag * later_real),
        )
    grad_sig = inverse(cos_table, sin_table, accum[0], accum[1], 0, block_rows)
    grad_signal = (grad_sig + skip_weight[None, :] * grad_mixed).astype(jnp.bfloat16)
    grad_pieces = []
    prior_real = None
    prior_imag = None
    for distance in range(lag_blocks):
        source_real, source_imag = sources[distance]
        corr_real = live_early[distance] * (dz_real * source_real + dz_imag * source_imag)
        corr_imag = live_early[distance] * (dz_imag * source_real - dz_real * source_imag)
        if distance > 0:
            grad_pieces.append(
                inverse(
                    cos_table,
                    sin_table,
                    alternate * prior_real + corr_real,
                    alternate * prior_imag + corr_imag,
                    0,
                    block_rows,
                )
            )
        prior_real = corr_real
        prior_imag = corr_imag
    grad_pieces.append(
        inverse(cos_table, sin_table, alternate * prior_real, alternate * prior_imag, 0, block_rows)
    )
    total_tokens = block_rows * lax.axis_size("seq")
    partial_grad = jnp.concatenate(grad_pieces, axis=0) * float(total_tokens) ** (-0.5)
    grad_filters = lax.psum_scatter(partial_grad, "seq", scatter_dimension=0, tiled=True)
    return (output, grad_signal, grad_gate, grad_filters)


def solution(mesh):
    placed = (P("seq", "tp"), P("seq", "tp"), P(None, "tp"), P("tp"), P(), P("seq", "tp"))
    return jax.shard_map(
        on_device,
        mesh=mesh,
        in_specs=placed,
        out_specs=(P("seq", "tp"), P("seq", "tp"), P("seq", "tp"), P("seq", "tp")),
        check_vma=False,
    )
```

profile of v0, /device:TPU:72, one launch (start us, length us, event | category | flops | bytes accessed | tf_op | source)
XLA Modules:
  0.0 633.3 jit_solution(10370556262607915893)
XLA Ops:
  7.2 3.6 collective-permute-start
  10.8 14.5 %collective-permute-start.6 = (bf16[128,512]{1,0:T(8,128)(2,1)}, bf16[128,512]{1,0:T(8,128)(2,1)}, u32[]{:S(2)}, u32[]{:S(2)}) collective-permute-start(bf16[128,512]{1,0:T(8,128)(2,1)} %param.6), channel_id=1, source_target_pairs={{0,56},{8,64},{16,72},{24,80},{32,88},{40,96},{48,104},{56,112},{6... | collective-permute-start | bytes 393224 | tf_op jit(solution)/shard_map/ppermute | solution.py:15
  25.3 6.0 collective-permute-start.5
  31.3 6.0 collective-permute-start.4
  37.3 7.3 %collective-permute-start.3 = (bf16[128,512]{1,0:T(8,128)(2,1)}, bf16[128,512]{1,0:T(8,128)(2,1)S(1)}, u32[]{:S(2)}, u32[]{:S(2)}) collective-permute-start(bf16[128,512]{1,0:T(8,128)(2,1)} %param.6), channel_id=1, source_target_pairs={{0,32},{8,40},{16,48},{24,56},{32,64},{40,72},{48,80},{56,88},{64,... | collective-permute-start | bytes 393224 | tf_op jit(solution)/shard_map/ppermute | solution.py:15
  76.3 2.9 multiply_add_fusion.9
  79.7 3.1 collective-permute-start.2
  85.3 5.1 collective-permute-start.1
  94.6 1.4 fusion.412
  99.2 2.1 fusion.186
  101.5 2.2 fusion.253
  103.8 10.2 %all-reduce = (f32[128]{0:T(128)S(1)}, f32[128]{0:T(128)S(1)}) all-reduce(f32[128]{0:T(128)S(1)} %get-tuple-element.5, f32[128]{0:T(128)S(1)} %get-tuple-element.4), channel_id=1, replica_groups=mesh['seq'=64,'tp'=8] {'tp'}, use_global_device_ids=true, to_apply=%region_3.4 | all-reduce | flops 256 | bytes 2048 | tf_op jit(solution)/shard_map/psum | solution.py:103
  114.0 1.9 multiply_convert_fusion
  116.3 1.9 subtract_multiply_fusion.5
  118.4 2.3 subtract_multiply_fusion
  136.1 1.6 broadcast_multiply_fusion
  137.7 4.3 collective-permute-done.12
  142.0 12.8 %collective-permute-start.7 = (bf16[128,512]{1,0:T(8,128)(2,1)S(1)}, bf16[128,512]{1,0:T(8,128)(2,1)S(1)}, u32[]{:S(2)}, u32[]{:S(2)}) collective-permute-start(bf16[128,512]{1,0:T(8,128)(2,1)S(1)} %get-tuple-element.31), channel_id=1, source_target_pairs={{8,0},{16,8},{24,16},{32,24},{40,32},{48,40},{56,48},{64,56},{72,6... | collective-permute-start | bytes 393224 | tf_op jit(solution)/shard_map/ppermute | solution.py:15
  157.4 1.6 collective-permute-start.13
  161.5 7.3 %collective-permute-done.10 = bf16[128,512]{1,0:T(8,128)(2,1)} collective-permute-done((bf16[128,512]{1,0:T(8,128)(2,1)S(1)}, bf16[128,512]{1,0:T(8,128)(2,1)}, u32[]{:S(2)}, u32[]{:S(2)}) %collective-permute-start.10) | collective-permute-done | bytes 131104 | tf_op jit(solution)/shard_map/ppermute | solution.py:15
  175.1 2.0 collective-permute-done.13
  177.9 1.9 fusion.108
  179.9 2.6 fusion.23
  182.5 444.0 %reduce-scatter.2.cloned.1.call-done = f32[16,512]{1,0:T(8,128)} async-done(((f32[1024,512]{1,0:T(8,128)}), f32[16,512]{1,0:T(8,128)}) %reduce-scatter.2.cloned.1.call-update) | async-done | bytes 32784 | tf_op jit(solution)/shard_map/reduce_scatter | solution.py:157
  (211 shorter events, 59.5 us)
Async XLA Ops:
  7.2 42.0 %copy-start.55 = (bf16[1024,512]{1,0:T(8,128)(2,1)S(1)}, bf16[1024,512]{1,0:T(8,128)(2,1)}, u32[]{:S(2)}) copy-start(bf16[1024,512]{1,0:T(8,128)(2,1)} %param.8) | copy-start | bytes 3145732
  7.2 619.3 %reduce-scatter.2.cloned.1.call-start = ((), (), s32[]{:S(2)}) async-start(), calls=%async_computation.1 | async-start | bytes 2129920 | tf_op jit(solution)/shard_map/reduce_scatter | solution.py:157
  7.2 72.4 %collective-permute-start = (bf16[128,512]{1,0:T(8,128)(2,1)}, bf16[128,512]{1,0:T(8,128)(2,1)}, u32[]{:S(2)}, u32[]{:S(2)}) collective-permute-start(bf16[128,512]{1,0:T(8,128)(2,1)} %param.6), channel_id=1, source_target_pairs={{0,8},{8,16},{16,24},{24,32},{32,40},{40,48},{48,56},{56,64},{64,7... | collective-permute-start | bytes 393224 | tf_op jit(solution)/shard_map/ppermute | solution.py:15
  10.8 74.5 %collective-permute-start.6 = (bf16[128,512]{1,0:T(8,128)(2,1)}, bf16[128,512]{1,0:T(8,128)(2,1)}, u32[]{:S(2)}, u32[]{:S(2)}) collective-permute-start(bf16[128,512]{1,0:T(8,128)(2,1)} %param.6), channel_id=1, source_target_pairs={{0,56},{8,64},{16,72},{24,80},{32,88},{40,96},{48,104},{56,112},{6... | collective-permute-start | bytes 393224 | tf_op jit(solution)/shard_map/ppermute | solution.py:15
  25.3 67.8 %collective-permute-start.5 = (bf16[128,512]{1,0:T(8,128)(2,1)}, bf16[128,512]{1,0:T(8,128)(2,1)}, u32[]{:S(2)}, u32[]{:S(2)}) collective-permute-start(bf16[128,512]{1,0:T(8,128)(2,1)} %param.6), channel_id=1, source_target_pairs={{0,48},{8,56},{16,64},{24,72},{32,80},{40,88},{48,96},{56,104},{64... | collective-permute-start | bytes 393224 | tf_op jit(solution)/shard_map/ppermute | solution.py:15
  31.3 64.7 %collective-permute-start.4 = (bf16[128,512]{1,0:T(8,128)(2,1)}, bf16[128,512]{1,0:T(8,128)(2,1)S(1)}, u32[]{:S(2)}, u32[]{:S(2)}) collective-permute-start(bf16[128,512]{1,0:T(8,128)(2,1)} %param.6), channel_id=1, source_target_pairs={{0,40},{8,48},{16,56},{24,64},{32,72},{40,80},{48,88},{56,96},{64,... | collective-permute-start | bytes 393224 | tf_op jit(solution)/shard_map/ppermute | solution.py:15
  37.3 59.4 %collective-permute-start.3 = (bf16[128,512]{1,0:T(8,128)(2,1)}, bf16[128,512]{1,0:T(8,128)(2,1)S(1)}, u32[]{:S(2)}, u32[]{:S(2)}) collective-permute-start(bf16[128,512]{1,0:T(8,128)(2,1)} %param.6), channel_id=1, source_target_pairs={{0,32},{8,40},{16,48},{24,56},{32,64},{40,72},{48,80},{56,88},{64,... | collective-permute-start | bytes 393224 | tf_op jit(solution)/shard_map/ppermute | solution.py:15
  59.2 42.0 %copy-start = (f32[256,512]{1,0:T(8,128)}, f32[256,512]{1,0:T(8,128)S(1)}, u32[]{:S(2)}) copy-start(f32[256,512]{1,0:T(8,128)S(1)} %convolution_negate_fusion.14) | copy-start | bytes 1572868
  59.6 41.6 %copy-start.2 = (f32[256,512]{1,0:T(8,128)}, f32[256,512]{1,0:T(8,128)S(1)}, u32[]{:S(2)}) copy-start(f32[256,512]{1,0:T(8,128)S(1)} %fusion.340) | copy-start | bytes 1572868
  79.2 22.1 %copy-start.8 = (f32[256,512]{1,0:T(8,128)}, f32[256,512]{1,0:T(8,128)S(1)}, u32[]{:S(2)}) copy-start(f32[256,512]{1,0:T(8,128)S(1)} %get-tuple-element.32) | copy-start | bytes 1572868
  79.2 22.1 %copy-start.10 = (f32[256,512]{1,0:T(8,128)}, f32[256,512]{1,0:T(8,128)S(1)}, u32[]{:S(2)}) copy-start(f32[256,512]{1,0:T(8,128)S(1)} %get-tuple-element.33) | copy-start | bytes 1572868
  79.2 22.1 %copy-start.12 = (f32[256,512]{1,0:T(8,128)}, f32[256,512]{1,0:T(8,128)S(1)}, u32[]{:S(2)}) copy-start(f32[256,512]{1,0:T(8,128)S(1)} %get-tuple-element.34) | copy-start | bytes 1572868
  79.2 22.1 %copy-start.14 = (f32[256,512]{1,0:T(8,128)}, f32[256,512]{1,0:T(8,128)S(1)}, u32[]{:S(2)}) copy-start(f32[256,512]{1,0:T(8,128)S(1)} %get-tuple-element.35) | copy-start | bytes 1572868
  79.2 22.1 %copy-start.16 = (f32[256,512]{1,0:T(8,128)}, f32[256,512]{1,0:T(8,128)S(1)}, u32[]{:S(2)}) copy-start(f32[256,512]{1,0:T(8,128)S(1)} %get-tuple-element.36) | copy-start | bytes 1572868
  79.2 22.1 %copy-start.18 = (f32[256,512]{1,0:T(8,128)}, f32[256,512]{1,0:T(8,128)S(1)}, u32[]{:S(2)}) copy-start(f32[256,512]{1,0:T(8,128)S(1)} %get-tuple-element.43) | copy-start | bytes 1572868
  79.7 17.9 %collective-permute-start.2 = (bf16[128,512]{1,0:T(8,128)(2,1)S(1)}, bf16[128,512]{1,0:T(8,128)(2,1)S(1)}, u32[]{:S(2)}, u32[]{:S(2)}) collective-permute-start(bf16[128,512]{1,0:T(8,128)(2,1)S(1)} %copy-done.57), channel_id=1, source_target_pairs={{0,24},{8,32},{16,40},{24,48},{32,56},{40,64},{48,72},{56,80},{64,... | collective-permute-start | bytes 393224 | tf_op jit(solution)/shard_map/ppermute | solution.py:15
  85.3 13.0 %collective-permute-start.1 = (bf16[128,512]{1,0:T(8,128)(2,1)S(1)}, bf16[128,512]{1,0:T(8,128)(2,1)S(1)}, u32[]{:S(2)}, u32[]{:S(2)}) collective-permute-start(bf16[128,512]{1,0:T(8,128)(2,1)S(1)} %copy-done.57), channel_id=1, source_target_pairs={{0,16},{8,24},{16,32},{24,40},{32,48},{40,56},{48,64},{56,72},{64,... | collective-permute-start | bytes 393224 | tf_op jit(solution)/shard_map/ppermute | solution.py:15
  125.1 16.9 %collective-permute-start.12 = (bf16[128,512]{1,0:T(8,128)(2,1)S(1)}, bf16[128,512]{1,0:T(8,128)(2,1)}, u32[]{:S(2)}, u32[]{:S(2)}) collective-permute-start(bf16[128,512]{1,0:T(8,128)(2,1)S(1)} %get-tuple-element.31), channel_id=1, source_target_pairs={{48,0},{56,8},{64,16},{72,24},{80,32},{88,40},{96,48},{104,56},{11... | collective-permute-start | bytes 393224 | tf_op jit(solution)/shard_map/ppermute | solution.py:15
  126.4 31.0 %collective-permute-start.11 = (bf16[128,512]{1,0:T(8,128)(2,1)S(1)}, bf16[128,512]{1,0:T(8,128)(2,1)}, u32[]{:S(2)}, u32[]{:S(2)}) collective-permute-start(bf16[128,512]{1,0:T(8,128)(2,1)S(1)} %get-tuple-element.31), channel_id=1, source_target_pairs={{40,0},{48,8},{56,16},{64,24},{72,32},{80,40},{88,48},{96,56},{104... | collective-permute-start | bytes 393224 | tf_op jit(solution)/shard_map/ppermute | solution.py:15
  127.7 41.1 %collective-permute-start.10 = (bf16[128,512]{1,0:T(8,128)(2,1)S(1)}, bf16[128,512]{1,0:T(8,128)(2,1)}, u32[]{:S(2)}, u32[]{:S(2)}) collective-permute-start(bf16[128,512]{1,0:T(8,128)(2,1)S(1)} %get-tuple-element.31), channel_id=1, source_target_pairs={{32,0},{40,8},{48,16},{56,24},{64,32},{72,40},{80,48},{88,56},{96,... | collective-permute-start | bytes 393224 | tf_op jit(solution)/shard_map/ppermute | solution.py:15
  129.0 43.8 %collective-permute-start.9 = (bf16[128,512]{1,0:T(8,128)(2,1)S(1)}, bf16[128,512]{1,0:T(8,128)(2,1)S(1)}, u32[]{:S(2)}, u32[]{:S(2)}) collective-permute-start(bf16[128,512]{1,0:T(8,128)(2,1)S(1)} %get-tuple-element.31), channel_id=1, source_target_pairs={{24,0},{32,8},{40,16},{48,24},{56,32},{64,40},{72,48},{80,56},{88,... | collective-permute-start | bytes 393224 | tf_op jit(solution)/shard_map/ppermute | solution.py:15
  130.3 43.2 %collective-permute-start.8 = (bf16[128,512]{1,0:T(8,128)(2,1)S(1)}, bf16[128,512]{1,0:T(8,128)(2,1)S(1)}, u32[]{:S(2)}, u32[]{:S(2)}) collective-permute-start(bf16[128,512]{1,0:T(8,128)(2,1)S(1)} %get-tuple-element.31), channel_id=1, source_target_pairs={{16,0},{24,8},{32,16},{40,24},{48,32},{56,40},{64,48},{72,56},{80,... | collective-permute-start | bytes 393224 | tf_op jit(solution)/shard_map/ppermute | solution.py:15
  142.0 32.3 %collective-permute-start.7 = (bf16[128,512]{1,0:T(8,128)(2,1)S(1)}, bf16[128,512]{1,0:T(8,128)(2,1)S(1)}, u32[]{:S(2)}, u32[]{:S(2)}) collective-permute-start(bf16[128,512]{1,0:T(8,128)(2,1)S(1)} %get-tuple-element.31), channel_id=1, source_target_pairs={{8,0},{16,8},{24,16},{32,24},{40,32},{48,40},{56,48},{64,56},{72,6... | collective-permute-start | bytes 393224 | tf_op jit(solution)/shard_map/ppermute | solution.py:15
  157.4 19.6 %collective-permute-start.13 = (bf16[128,512]{1,0:T(8,128)(2,1)S(1)}, bf16[128,512]{1,0:T(8,128)(2,1)S(1)}, u32[]{:S(2)}, u32[]{:S(2)}) collective-permute-start(bf16[128,512]{1,0:T(8,128)(2,1)S(1)} %get-tuple-element.31), channel_id=1, source_target_pairs={{56,0},{64,8},{72,16},{80,24},{88,32},{96,40},{104,48},{112,56},{1... | collective-permute-start | bytes 393224 | tf_op jit(solution)/shard_map/ppermute | solution.py:15
  (53 other events, 323.0 us)
Sparse Core Ops, SparseCore 0:
  137.9 488.5 reduce-scatter.1
where the time goes:
time: 634 us; the launch traced here: 633 us
  waiting for transfers between devices  459 us (72%)
  starting transfers between devices  66.5 us (10%)
  matrix products  61.2 us (10%)
  between operations  25.3 us (4%)
  other arithmetic  10.3 us (2%)
  blocking collectives  10.2 us (2%)
    reduce_scatter x1, waiting for transfers between devices, on_device(): lax.psum_scatter(partial_grad, 'seq', scatter_dimension=0, tiled=True)  444 us
    ppermute x14, starting transfers between devices, from_behind(): lax.ppermute(value, axis, [(source, source + steps) for source in range(i...  66.5 us
    dot_general x68, matrix products, product(): jnp.dot(matrix, values, precision=HIGHEST, preferred_element_type=jnp.flo...  61.2 us
    ppermute x14, waiting for transfers between devices, from_behind(): lax.ppermute(value, axis, [(source, source + steps) for source in range(i...  14.8 us
  transfers between devices with their start and end apart: 15, of which 5 were waited for; matrix products, arithmetic and copies ran while one was open for 9% of the time, Pallas kernels for 0%

commit v1 on v0

v1 whole, which is shorter than its diff:
```python
import functools
import math

import jax
import jax.numpy as jnp
import numpy as np
from jax import lax
from jax.experimental import pallas as pl
from jax.experimental.pallas import tpu as pltpu
from jax.sharding import PartitionSpec as P

EPSILON = 1e-06
MESH = pl.DeviceIdType.MESH
T = 128
C = 128
Q = 4
LAGS = 8
REL = 20
F32 = jnp.float32
BF16 = jnp.bfloat16


def tables():
    freq = np.arange(T)[:, None]
    time = np.arange(2 * T)[None, :]
    phase = (freq * time % (2 * T)) * (2.0 * math.pi / (2 * T))
    real, imag = np.cos(phase), -np.sin(phase)
    imag[0] = 1 - 2 * (np.arange(2 * T) % 2)
    forward = np.concatenate([real, imag], axis=0)
    scale = np.full((2 * T, 1), 1.0 / T)
    scale[0] = scale[T] = 0.5 / T
    backward = (forward * scale).T

    def split(table):
        table = table.astype(np.float32)
        high = table.astype(jnp.bfloat16)
        low = (table - high.astype(np.float32)).astype(jnp.bfloat16)
        return high, low

    high, low = split(forward)
    first = np.concatenate([high[:, :T], low[:, :T]], axis=1)
    second = np.concatenate([high[:, T:], low[:, T:]], axis=1)
    back_high, back_low = split(backward)
    return np.stack([first, second, back_high, back_low])


def dot(a, b):
    return jnp.dot(a, b, preferred_element_type=F32)


def kernel(
    docs, skip, signal, gate, filters, cotangent, table,
    out, gsig, ggate, gfilt,
    sig_v, gate_v, cot_v, taps, tab, xbuf, dbuf, spec, dspec, kr, ki, kn, prod, gprod,
    conv_s, conv_r, back_s, back_r, zval, dz, tpbuf, gf_s, gf_r, gx_s, gx_r, gz_s, gz_r,
    load_sem, za_s, za_r, yf_s, yf_r, xh_s, xh_r, zb_s, zb_r, tp_s, tp_r,
    da_s, da_r, df_s, df_r, dh_s, dh_r, db_s, db_r, gy_ss, gy_rs, gx_ss, gx_rs, gz_ss, gz_rs,
):
    seq, tpi = lax.axis_index("seq"), lax.axis_index("tp")
    x, z, y = seq // 16, (seq // 4) % 4, seq % 4

    def at(xx, zz, yy):
        return (lax.rem(xx, Q) * 16 + lax.rem(zz, Q) * 4 + lax.rem(yy, Q), tpi)

    def send(src, dst, ssem, rsem, target):
        return pltpu.make_async_remote_copy(
            src_ref=src, dst_ref=dst, send_sem=ssem, recv_sem=rsem, device_id=target, device_id_type=MESH
        )

    barrier = pltpu.get_barrier_semaphore()
    partners = [at(x, z + k, y) for k in (2, 1, 3)] + [at(x, z, y + k) for k in (1, 2, 3)]
    partners += [at(x + i, z, y + k) for i in (1, 3) for k in range(Q)] + [at(x + 2, z, y)]
    partners += [(seq, lax.rem(tpi + k, 8)) for k in range(1, 8)]
    for partner in partners:
        pl.semaphore_signal(barrier, inc=1, device_id=partner, device_id_type=MESH)

    lanes = pl.ds(pl.multiple_of(z * C, C), C)
    loads = [
        pltpu.make_async_copy(table, tab, load_sem.at[0]),
        pltpu.make_async_copy(filters.at[:, lanes], taps, load_sem.at[1]),
        pltpu.make_async_copy(signal, sig_v, load_sem.at[2]),
        pltpu.make_async_copy(gate, gate_v, load_sem.at[3]),
        pltpu.make_async_copy(cotangent, cot_v, load_sem.at[4]),
    ]
    for load in loads:
        load.start()

    early, late = [], []
    for zp in range(Q):
        block = 16 * x + 4 * zp + y
        begin, first, last = jnp.int32(0), jnp.int32(0), jnp.int32(0)
        for k in range(docs.shape[0]):
            end = begin + docs[k]
            inside = (begin <= block) & (block < end)
            first = jnp.where(inside, begin, first)
            last = jnp.where(inside, end, last)
            begin = end
        early.append([jnp.where(block - d >= first, 1.0, 0.0).astype(F32) for d in range(LAGS)])
        late.append([jnp.where(block + d < last, 1.0, 0.0).astype(F32) for d in range(LAGS)])

    row0 = lax.broadcasted_iota(jnp.int32, (T, C), 0) == 0
    loads[0].wait()
    loads[1].wait()
    for d in range(LAGS):
        tap = taps[d * T : (d + 1) * T, :]
        value = dot(tab[1], jnp.concatenate([tap, tap], axis=0))
        if d > 0:
            before = taps[(d - 1) * T : d * T, :]
            value += dot(tab[0], jnp.concatenate([before, before], axis=0))
        real, imag = value[:T], value[T:]
        kr[d] = real
        ki[d] = jnp.where(row0, 0.0, imag)
        kn[d] = jnp.where(row0, imag, real)
    for load in loads[2:]:
        load.wait()
    pl.semaphore_wait(barrier, len(partners))

    def chunk(k):
        return pl.ds(pl.multiple_of(lax.rem(k, Q) * C, C), C)

    def spread(source, buf, shift, xstep, za_s, za_r, yf_s, yf_r, xh_s, xh_r):
        waits = []
        own = shift + 4 * z + y
        for k in (2, 1, 3):
            copy = send(source.at[:, chunk(z + k)], buf.at[own], za_s.at[k - 1], za_r.at[k - 1], at(x, z + k, y))
            copy.start()
            waits.append(copy)
        buf[own] = source[:, lanes]
        forward = xstep == 1
        halo_shift = 0 if forward else 16
        sent = []
        for k in (0, 1, 3, 2):
            zsrc = lax.rem(z + 4 - k, Q)
            if k:
                send(source.at[:, lanes], buf.at[shift + 4 * zsrc + y], za_s.at[k - 1], za_r.at[k - 1], at(x, z, y)).wait_recv()
            slot = buf.at[shift + 4 * zsrc + y]
            far, near = (zsrc == 3, zsrc == 2) if forward else (zsrc == 0, zsrc == 1)
            for j in (2, 1, 3, 0):
                yp = lax.rem(y + j, Q)
                ahead = yp > y if forward else yp < y
                if j:
                    needed = jnp.logical_not(far) | ahead
                    copy = send(slot, slot, yf_s.at[k, j - 1], yf_r.at[zsrc, j - 1], at(x, z, yp))
                    pl.when(needed)(copy.start)
                    sent.append((needed, copy))
                behind = yp < y if forward else yp > y
                needed = far | (near & behind)
                side = jnp.where(far, 1, 0)
                hslot = buf.at[halo_shift + lax.rem(4 * zsrc + 8, 16) % 8 + y]
                copy = send(slot, hslot, xh_s.at[k, j], xh_r.at[side, j], at(x + xstep, z, yp))
                pl.when(needed)(copy.start)
                sent.append((needed, copy))
        for zsrc in range(Q):
            for j in (1, 2, 3):
                ysrc = lax.rem(y + 4 - j, Q)
                slot = buf.at[shift + 4 * zsrc + ysrc]
                copy = send(slot, slot, yf_s.at[0, j - 1], yf_r.at[zsrc, j - 1], at(x, z, ysrc))
                if zsrc == (3 if forward else 0):
                    pl.when(y > ysrc if forward else y < ysrc)(copy.wait_recv)
                else:
                    copy.wait_recv()
        for side in (0, 1):
            for j in range(Q):
                ysrc = lax.rem(y + 4 - j, Q)
                quad = (2 + side) if forward else (1 - side)
                slot = buf.at[halo_shift + (4 * quad) % 8 + ysrc]
                copy = send(slot, slot, xh_s.at[0, j], xh_r.at[side, j], at(x + 4 - xstep, z, ysrc))
                if side:
                    copy.wait_recv()
                else:
                    pl.when(y < ysrc if forward else y > ysrc)(copy.wait_recv)
        return waits, sent

    def transform(tbl, buf, start, count, result):
        def body(i, _):
            pair = buf[pl.ds(start + 2 * i, 2)]
            wide = jnp.concatenate([pair[0], pair[1]], axis=1)
            value = dot(tab[tbl], jnp.concatenate([wide, wide], axis=0))
            result[2 * i] = value[:, :C]
            result[2 * i + 1] = value[:, C:]
            return 0

        lax.fori_loop(0, count // 2, body, 0)

    def inverse(rows, values):
        high = values.astype(BF16)
        low = (values - high.astype(F32)).astype(BF16)
        vh, vl = tab[2, rows, :], tab[3, rows, :]
        return dot(vh, high) + dot(vh, low) + dot(vl, high)

    def tile(f):
        return pl.ds(pl.multiple_of(8 * f, 8), 8), pl.ds(pl.multiple_of(T + 8 * f, 8), 8)

    sends = []
    waits, sent = spread(sig_v, xbuf, 8, 1, za_s, za_r, yf_s, yf_r, xh_s, xh_r)
    sends.append((waits, sent))
    transform(0, xbuf, 1 + y, REL, spec)

    def forward_tile(f, _):
        re, im = tile(f)
        for zp in range(Q):
            acc_r = jnp.zeros((8, C), F32)
            acc_i = jnp.zeros((8, C), F32)
            for d in range(LAGS):
                r = 7 + 4 * zp - d
                live = early[zp][d]
                s_r, s_i = spec[r, re, :] * live, spec[r, im, :] * live
                acc_r += kr[d, re, :] * s_r - ki[d, re, :] * s_i
                acc_i += kn[d, re, :] * s_i + ki[d, re, :] * s_r
            prod[re, zp * C : (zp + 1) * C] = acc_r
            prod[im, zp * C : (zp + 1) * C] = acc_i
        return 0

    lax.fori_loop(0, T // 8, forward_tile, 0)

    def give_back(rows, sbuf, rbuf, ssem, rsem):
        value = inverse(rows, prod[...]).astype(BF16)
        for zp in range(Q):
            sbuf[zp] = value[:, zp * C : (zp + 1) * C]
        copies = []
        for k in (2, 1, 3):
            copy = send(sbuf.at[lax.rem(z + k, Q)], rbuf.at[z], ssem.at[k - 1], rsem.at[k - 1], at(x, z + k, y))
            copy.start()
            copies.append(copy)
        rbuf[z] = sbuf[z]
        return copies

    copies = give_back(slice(T, 2 * T), conv_s, conv_r, zb_s, zb_r)
    for k in (1, 3, 2):
        copies[(2, 1, 3).index(k)].wait_recv()
    sends.append((copies, []))

    squares = jnp.zeros((T, C), F32)
    dots = jnp.zeros((T, C), F32)
    for j in range(Q):
        cols = slice(j * C, (j + 1) * C)
        mixed = conv_r[j].astype(F32) + skip[:, cols] * sig_v[:, cols].astype(F32)
        zval[:, cols] = mixed
        gated = gate_v[:, cols].astype(F32) * mixed
        squares += gated * gated
        dots += cot_v[:, cols].astype(F32) * gated

    ones = jnp.ones((8, C), BF16)

    def row_sums(values):
        total = jnp.zeros((8, T), F32)
        for _ in range(3):
            part = values.astype(BF16)
            total += lax.dot_general(ones, part, (((1,), (1,)), ((), ())), preferred_element_type=F32)
            values = values - part.astype(F32)
        return total

    upper = lax.broadcasted_iota(jnp.int32, (8, T), 0) < 4
    tpbuf[0] = jnp.where(upper, row_sums(squares), row_sums(dots))
    copies = []
    for k in range(1, 8):
        copy = send(tpbuf.at[0], tpbuf.at[k], tp_s.at[k - 1], tp_r.at[k - 1], (seq, lax.rem(tpi + k, 8)))
        copy.start()
        copies.append(copy)
    for copy in copies:
        copy.wait_recv()
    sends.append((copies, []))
    total = jnp.zeros((8, T), F32)
    for k in range(8):
        total += tpbuf[lax.rem(tpi + 8 - k, 8)]
    mean = total / (4 * C * 8)
    inv_row = lax.rsqrt(mean[0:1] + EPSILON)
    fac_row = mean[4:5] * inv_row * inv_row * inv_row
    inv = jnp.broadcast_to(inv_row, (T, T)).T
    fac = jnp.broadcast_to(fac_row, (T, T)).T
    for j in range(Q):
        cols = slice(j * C, (j + 1) * C)
        mixed = zval[:, cols]
        gate_f = gate_v[:, cols].astype(F32)
        gated = gate_f * mixed
        dgated = cot_v[:, cols].astype(F32) * inv - gated * fac
        dz[:, cols] = (dgated * gate_f).astype(BF16)
        out[:, cols] = (gated * inv).astype(BF16)
        ggate[:, cols] = (dgated * mixed).astype(BF16)

    waits, sent = spread(dz, dbuf, 0, 3, da_s, da_r, df_s, df_r, dh_s, dh_r)
    sends.append((waits, sent))
    transform(1, dbuf, y, REL, dspec)

    def filter_tile(f, _):
        re, im = tile(f)
        first = (lax.broadcasted_iota(jnp.int32, (8, C), 0) == 0) & (f == 0)
        sign = (1 - 2 * (lax.broadcasted_iota(jnp.int32, (8, C), 0) % 2)).astype(F32)
        own = []
        for zp in range(Q):
            d_r, d_i = dspec[4 * zp, re, :], dspec[4 * zp, im, :]
            own.append((d_r, jnp.where(first, 0.0, d_i), jnp.where(first, -d_i, d_r)))
        prior = None
        for d in range(LAGS):
            acc_r = jnp.zeros((8, C), F32)
            acc_i = jnp.zeros((8, C), F32)
            for zp in range(Q):
                r = 7 + 4 * zp - d
                live = early[zp][d]
                s_r, s_i = spec[r, re, :] * live, spec[r, im, :] * live
                d_r, d_i, d_n = own[zp]
                acc_r += d_r * s_r + d_i * s_i
                acc_i += d_i * s_r - d_n * s_i
            if prior is not None:
                cols = slice((d - 1) * C, d * C)
                gprod[re, cols] = prior[0] * sign + acc_r
                gprod[im, cols] = prior[1] * sign + acc_i
            prior = (acc_r, acc_i)
        cols = slice((LAGS - 1) * C, LAGS * C)
        gprod[re, cols] = prior[0] * sign
        gprod[im, cols] = prior[1] * sign
        return 0

    lax.fori_loop(0, T // 8, filter_tile, 0)
    scale = float(64 * T) ** (-0.5)
    for d in range(LAGS):
        value = inverse(slice(0, T), gprod[:, d * C : (d + 1) * C]) * scale
        for i in range(8):
            gf_s[i % 4, (d // 2) * 4 + 2 * (d % 2) + i // 4] = value[16 * i : 16 * i + 16].astype(BF16)
    gy_copies = []
    for k in (2, 1, 3):
        copy = send(gf_s.at[lax.rem(y + k, Q)], gf_r.at[k - 1], gy_ss.at[k - 1], gy_rs.at[k - 1], at(x, z, y + k))
        copy.start()
        gy_copies.append(copy)

    def backward_tile(f, _):
        re, im = tile(f)
        for zp in range(Q):
            acc_r = jnp.zeros((8, C), F32)
            acc_i = jnp.zeros((8, C), F32)
            for d in range(LAGS):
                r = 4 * zp + d
                live = late[zp][d]
                s_r, s_i = dspec[r, re, :] * live, dspec[r, im, :] * live
                acc_r += kr[d, re, :] * s_r + ki[d, re, :] * s_i
                acc_i += kn[d, re, :] * s_i - ki[d, re, :] * s_r
            prod[re, zp * C : (zp + 1) * C] = acc_r
            prod[im, zp * C : (zp + 1) * C] = acc_i
        return 0

    lax.fori_loop(0, T // 8, backward_tile, 0)
    back_copies = give_back(slice(0, T), back_s, back_r, db_s, db_r)
    sends.append((back_copies, []))

    for copy in gy_copies:
        copy.wait_recv()
    sends.append((gy_copies, []))
    gx_s[...] = (
        gf_s[y].astype(F32) + gf_r[0].astype(F32) + gf_r[1].astype(F32) + gf_r[2].astype(F32)
    ).reshape(Q, 4, 16, C)
    gx_copies = []
    for k in (2, 1, 3):
        copy = send(gx_s.at[lax.rem(x + k, Q)], gx_r.at[k - 1], gx_ss.at[k - 1], gx_rs.at[k - 1], at(x + k, z, y))
        copy.start()
        gx_copies.append(copy)
    for copy in gx_copies:
        copy.wait_recv()
    sends.append((gx_copies, []))
    gz_s[...] = gx_s[x] + gx_r[0] + gx_r[1] + gx_r[2]
    gz_copies = []
    for k in (2, 1, 3):
        copy = send(gz_s.at[lax.rem(z + k, Q)], gz_r.at[z], gz_ss.at[k - 1], gz_rs.at[k - 1], at(x, z + k, y))
        copy.start()
        gz_copies.append(copy)
    sends.append((gz_copies, []))
    gz_r[z] = gz_s[z]

    for copy in back_copies:
        copy.wait_recv()
    for j in range(Q):
        cols = slice(j * C, (j + 1) * C)
        gsig[:, cols] = (back_r[j].astype(F32) + skip[:, cols] * dz[:, cols].astype(F32)).astype(BF16)
    for copy in gz_copies:
        copy.wait_recv()
    for j in range(Q):
        gfilt[:, j * C : (j + 1) * C] = gz_r[j]

    for copies, conditional in sends:
        for copy in copies:
            copy.wait_send()
        for needed, copy in conditional:
            pl.when(needed)(copy.wait_send)


def on_device(signal, gate_input, filters, skip_weight, doc_lengths, grad_out):
    channels = signal.shape[1]
    vmem, anywhere = pl.BlockSpec(memory_space=pltpu.VMEM), pl.BlockSpec(memory_space=pl.ANY)
    dma = lambda *shape: pltpu.SemaphoreType.DMA(shape)
    block = (T, channels)
    scratch = [
        pltpu.VMEM(block, BF16), pltpu.VMEM(block, BF16), pltpu.VMEM(block, BF16),
        pltpu.VMEM((LAGS * T, C), BF16), pltpu.VMEM((4, 2 * T, 2 * T), BF16),
        pltpu.VMEM((24, T, C), BF16), pltpu.VMEM((24, T, C), BF16),
        pltpu.VMEM((REL, 2 * T, C), F32), pltpu.VMEM((REL, 2 * T, C), F32),
        pltpu.VMEM((LAGS, T, C), F32), pltpu.VMEM((LAGS, T, C), F32), pltpu.VMEM((LAGS, T, C), F32),
        pltpu.VMEM((2 * T, Q * C), F32), pltpu.VMEM((2 * T, LAGS * C), F32),
        pltpu.VMEM((Q, T, C), BF16), pltpu.VMEM((Q, T, C), BF16),
        pltpu.VMEM((Q, T, C), BF16), pltpu.VMEM((Q, T, C), BF16),
        pltpu.VMEM(block, F32), pltpu.VMEM(block, BF16), pltpu.VMEM((8, 8, T), F32),
        pltpu.VMEM((Q, 16, 16, C), BF16), pltpu.VMEM((3, 16, 16, C), BF16),
        pltpu.VMEM((Q, 4, 16, C), F32), pltpu.VMEM((3, 4, 16, C), F32),
        pltpu.VMEM((4, 16, C), F32), pltpu.VMEM((4, 16, C), F32),
        dma(5), dma(3), dma(3), dma(4, 3), dma(4, 3), dma(4, 4), dma(2, 4), dma(3), dma(3), dma(7), dma(7),
        dma(3), dma(3), dma(4, 3), dma(4, 3), dma(4, 4), dma(2, 4), dma(3), dma(3),
        dma(3), dma(3), dma(3), dma(3), dma(3), dma(3),
    ]
    out, gsig, ggate, gfilt = pl.pallas_call(
        kernel,
        out_shape=(
            jax.ShapeDtypeStruct(block, BF16), jax.ShapeDtypeStruct(block, BF16),
            jax.ShapeDtypeStruct(block, BF16), jax.ShapeDtypeStruct((16, channels), F32),
        ),
        in_specs=[pl.BlockSpec(memory_space=pltpu.SMEM), vmem] + [anywhere] * 5,
        out_specs=(vmem,) * 4,
        scratch_shapes=scratch,
        compiler_params=pltpu.CompilerParams(
            collective_id=0, has_side_effects=True, vmem_limit_bytes=48 << 20
        ),
        name="hyena",
    )(doc_lengths, skip_weight[None, :], signal, gate_input, filters, grad_out, jnp.asarray(tables()))
    return out, gsig, ggate, gfilt


def solution(mesh):
    placed = (P("seq", "tp"), P("seq", "tp"), P(None, "tp"), P("tp"), P(), P("seq", "tp"))
    return jax.shard_map(
        on_device,
        mesh=mesh,
        in_specs=placed,
        out_specs=(P("seq", "tp"), P("seq", "tp"), P("seq", "tp"), P("seq", "tp")),
        check_vma=False,
    )
```

time: 634 us -> 93.7 us (0.15)
  the two profiles are of different devices: /device:TPU:72 before, /device:TPU:8 now
where the time goes in v1:
time: 93.7 us; the launch traced here: 93.4 us
  Pallas kernels  83.8 us (89%)
  local copies, waits for them, and re-layouts  8.89 us (9%)
    pallas_call x1, Pallas kernels, on_device(): pl.pallas_call(kernel, out_shape=(jax.ShapeDtypeStruct(block, BF16), jax....  83.8 us
    unnamed x18, local copies, waits for them, and re-layouts  8.89 us

profile of v1, /device:TPU:8, one launch (start us, length us, event | category | flops | bytes accessed | tf_op | source)
XLA Modules:
  0.0 93.4 jit_solution(14961120952956262208)
XLA Ops:
  0.6 0.0 copy-start.6
  0.6 0.6 copy-done.6
  1.3 0.0 copy-start
  1.3 1.2 %copy-done = bf16[1024,512]{1,0:T(8,128)(2,1)S(1)} copy-done((bf16[1024,512]{1,0:T(8,128)(2,1)S(1)}, bf16[1024,512]{1,0:T(8,128)(2,1)}, u32[]{:S(2)}) %copy-start) | copy-done | bytes 1048600
  2.5 0.0 copy-start.1
  2.5 1.0 %copy-done.1 = bf16[4,256,256]{2,1,0:T(8,128)(2,1)S(1)} copy-done((bf16[4,256,256]{2,1,0:T(8,128)(2,1)S(1)}, bf16[4,256,256]{2,1,0:T(8,128)(2,1)}, u32[]{:S(2)}) %copy-start.1) | copy-done | bytes 524312
  3.6 0.0 copy-start.2
  3.6 0.9 copy-done.2
  4.5 0.0 copy-start.3
  4.5 0.9 copy-done.3
  5.4 0.0 copy-start.4
  5.4 0.9 copy-done.4
  6.3 0.0 copy-start.5
  6.3 0.7 copy-done.5
  7.0 83.8 %hyena.1 = (bf16[128,512]{1,0:T(8,128)(2,1)S(1)}, bf16[128,512]{1,0:T(8,128)(2,1)S(1)}, bf16[128,512]{1,0:T(8,128)(2,1)S(1)}, f32[16,512]{1,0:T(8,128)S(1)}) custom-call(s32[16]{0:T(128)S(1)} %copy-done.6, f32[1,512]{1,0:T(1,128)S(1)} %bitcast.1, bf16[128,512]{1,0:T(8,128)(2,1)S(1)} %copy-done.2, bf16[128,512]{1,0:T(8,128)(2,1)S(1)} %copy-done.3, ...), custom_call_target="tpu_custom_call" | custom-call | tf_op jit(solution)/shard_map/hyena/pallas_call | solution.py:407
  90.8 0.7 copy.15
  91.4 0.7 copy.16
  92.1 0.7 copy.17
  92.7 0.6 copy.18
Async XLA Ops:
  0.6 0.7 copy-start.6
  1.3 1.2 %copy-start = (bf16[1024,512]{1,0:T(8,128)(2,1)S(1)}, bf16[1024,512]{1,0:T(8,128)(2,1)}, u32[]{:S(2)}) copy-start(bf16[1024,512]{1,0:T(8,128)(2,1)} %filters.1) | copy-start | bytes 3145732
  2.5 1.0 %copy-start.1 = (bf16[4,256,256]{2,1,0:T(8,128)(2,1)S(1)}, bf16[4,256,256]{2,1,0:T(8,128)(2,1)}, u32[]{:S(2)}) copy-start(bf16[4,256,256]{2,1,0:T(8,128)(2,1)} %constant.2.clone.table) | copy-start | bytes 1572868
  3.6 0.9 copy-start.2
  4.5 0.9 copy-start.3
  5.4 0.9 copy-start.4
  6.3 0.7 copy-start.5

commit v2 on v1

v2 whole, which is shorter than its diff:
```python
import functools
import math

import jax
import jax.numpy as jnp
import numpy as np
from jax import lax
from jax.experimental import pallas as pl
from jax.experimental.pallas import tpu as pltpu
from jax.sharding import PartitionSpec as P

EPSILON = 1e-06
MESH = pl.DeviceIdType.MESH
T = 128
C = 128
Q = 4
LAGS = 8
REL = 20
F32 = jnp.float32
BF16 = jnp.bfloat16


def tables():
    freq = np.arange(T)[:, None]
    time = np.arange(2 * T)[None, :]
    phase = (freq * time % (2 * T)) * (2.0 * math.pi / (2 * T))
    real, imag = np.cos(phase), -np.sin(phase)
    imag[0] = 1 - 2 * (np.arange(2 * T) % 2)
    forward = np.concatenate([real, imag], axis=0)
    scale = np.full((2 * T, 1), 1.0 / T)
    scale[0] = scale[T] = 0.5 / T
    backward = (forward * scale).T

    def split(table):
        table = table.astype(np.float32)
        high = table.astype(jnp.bfloat16)
        low = (table - high.astype(np.float32)).astype(jnp.bfloat16)
        return high, low

    high, low = split(forward)
    first = np.concatenate([high[:, :T], low[:, :T]], axis=1)
    second = np.concatenate([high[:, T:], low[:, T:]], axis=1)
    back_high, back_low = split(backward)
    return np.stack([first, second, back_high, back_low])


def dot(a, b):
    return jnp.dot(a, b, preferred_element_type=F32)


def kernel(
    docs, skip, signal, gate, filters, cotangent, table,
    out, gsig, ggate, gfilt,
    docs_v, late_m, skip_v, sig_v, gate_v, cot_v, taps, tab, xbuf, gbuf, cbuf, dbuf, rbuf, spec, dspec, kr, ki, kn,
    prod, gprod, zval, out_s, ggate_s, gsig_s, own_r, near_r, wide_s, wide_r,
    gf_s, gf_r, gy_s, gy_r, gz_s,
    inside_sem, load_sem, za_s, za_r, zr_s, zr_r, zf_s, zf_r, ga_s, ga_r, ca_s, ca_r, yf_s, yf_r, xh_s, xh_r, p_ss, p_rs, n_ss, n_rs, w_ss, w_rs,
    df_s, df_r, dh_s, dh_r, ob_s, ob_r, gb_s, gb_r, sb_s, sb_r, gx_ss, gx_rs, gy_ss, gy_rs, gz_ss, gz_rs,
):
    seq, tpi = lax.axis_index("seq"), lax.axis_index("tp")
    x, z, y = seq // 16, (seq // 4) % 4, seq % 4

    def at(xx, zz, yy):
        return (lax.rem(xx, Q) * 16 + lax.rem(zz, Q) * 4 + lax.rem(yy, Q), tpi)

    def send(src, dst, ssem, rsem, target):
        return pltpu.make_async_remote_copy(
            src_ref=src, dst_ref=dst, send_sem=ssem, recv_sem=rsem, device_id=target, device_id_type=MESH
        )

    barrier = pltpu.get_barrier_semaphore()
    partners = [at(x, z + k, y) for k in (1, 3)] + [at(x, z, y + k) for k in (1, 2, 3)]
    partners += [at(x + i, z, y + k) for i in (1, 3) for k in range(Q)] + [at(x + 2, z, y)]
    place, core = 4 * z + tpi // 2, lax.rem(tpi, 2)

    def ring(step, other):
        spot = lax.rem(place + step + 16, 16)
        return (16 * x + 4 * (spot // 4) + y, 2 * lax.rem(spot, 4) + lax.rem(core + other, 2))

    near = (8, 2, -2, 1, -1)
    wide = (5, -5)
    partners += [ring(step, 0) for step in near[1:]] + [ring(0, 1)]
    for partner in partners:
        pl.semaphore_signal(barrier, inc=1, device_id=partner, device_id_type=MESH)

    def chunk(k):
        return pl.ds(pl.multiple_of(lax.rem(k, Q) * C, C), C)

    lanes = chunk(z)
    own = 8 + 4 * z + y
    loads = [
        pltpu.make_async_copy(docs, docs_v, load_sem.at[0]),
        pltpu.make_async_copy(filters.at[:, lanes], taps, load_sem.at[1]),
        pltpu.make_async_copy(table, tab, load_sem.at[2]),
        pltpu.make_async_copy(signal, sig_v, load_sem.at[3]),
        pltpu.make_async_copy(signal.at[:, lanes], xbuf.at[own], load_sem.at[4]),
        pltpu.make_async_copy(gate.at[:, lanes], gbuf.at[z], load_sem.at[5]),
        pltpu.make_async_copy(cotangent.at[:, lanes], cbuf.at[z], load_sem.at[6]),
        pltpu.make_async_copy(skip.at[:, lanes], skip_v, load_sem.at[7]),
        pltpu.make_async_copy(gate, gate_v, load_sem.at[8]),
        pltpu.make_async_copy(cotangent, cot_v, load_sem.at[9]),
    ]
    for load in loads:
        load.start()

    for load in loads[3:]:
        load.wait()
    pl.semaphore_wait(barrier, len(partners))

    def along_z(source, target, ssem, rsem):
        copies = {}
        for k in (2, 1, 3):
            copies[k] = send(source.at[:, chunk(z + k)], target, ssem.at[k - 1], rsem.at[k - 1], at(x, z + k, y))
            copies[k].start()
        return copies

    def back_along_z(source, result, ssem, rsem):
        copies = {}
        for k in (2, 1, 3):
            copies[k] = send(
                source.at[lax.rem(z + k, Q)], result.at[:, lanes], ssem.at[k - 1], rsem.at[k - 1], at(x, z + k, y)
            )
            copies[k].start()
        result[:, lanes] = source[z]
        return copies

    def transform(tbl, buf, start, count, result):
        def body(i, _):
            pair = buf[pl.ds(start + 2 * i, 2)]
            wide = jnp.concatenate([pair[0], pair[1]], axis=1)
            value = dot(tab[tbl], jnp.concatenate([wide, wide], axis=0))
            result[start + 2 * i] = value[:, :C]
            result[start + 2 * i + 1] = value[:, C:]
            return 0

        lax.fori_loop(0, count // 2, body, 0)

    def inverse(rows, values):
        high = values.astype(BF16)
        low = (values - high.astype(F32)).astype(BF16)
        vh, vl = tab[2, rows, :], tab[3, rows, :]
        return dot(vh, high) + dot(vh, low) + dot(vl, high)

    def tile(f):
        return pl.ds(pl.multiple_of(8 * f, 8), 8), pl.ds(pl.multiple_of(T + 8 * f, 8), 8)

    waits = []
    halves = (pl.ds(0, T // 2), pl.ds(T // 2, T // 2))
    steps = (1, 3)
    relays = []
    for h, k in enumerate(steps):
        copy = send(sig_v.at[halves[h], chunk(z + 2)], rbuf.at[h], zr_s.at[h], zr_r.at[h], at(x, z + k, y))
        copy.start()
        relays.append(copy)
    for k in steps:
        copy = send(sig_v.at[:, chunk(z + k)], xbuf.at[own], za_s.at[k - 1], za_r.at[k - 1], at(x, z + k, y))
        copy.start()
        waits.append(copy)
    waits += relays
    for k in steps:
        pl.semaphore_signal(inside_sem, inc=1, device_id=at(x, z + k, y), device_id_type=MESH)
    sent = []
    late_loads = []

    def arrivals(zsrc):
        for j in (1, 2, 3):
            ysrc = lax.rem(y + 4 - j, Q)
            slot = xbuf.at[8 + 4 * zsrc + ysrc]
            copy = send(slot, slot, yf_s.at[0, j - 1], yf_r.at[zsrc, j - 1], at(x, z, ysrc))
            pl.when((zsrc < 3) | (y > ysrc))(copy.wait_recv)

    earlier = None
    for k in (0, 1, 3, 2):
        zsrc = lax.rem(z + 4 - k, Q)
        slot = xbuf.at[8 + 4 * zsrc + y]
        if k == 2:
            for h in range(2):
                half = slot.at[halves[h]]
                send(half, half, zf_s.at[h], zf_r.at[h], at(x, z + 2, y)).wait_recv()
        elif k:
            send(slot, slot, za_s.at[k - 1], za_r.at[k - 1], at(x, z + k, y)).wait_recv()
        for j in (2, 1, 3, 0):
            yp = lax.rem(y + j, Q)
            if j:
                needed = (zsrc < 3) | (yp > y)
                copy = send(slot, slot, yf_s.at[k, j - 1], yf_r.at[zsrc, j - 1], at(x, z, yp))
                pl.when(needed)(copy.start)
                sent.append((needed, copy))
            needed = (zsrc == 3) | ((zsrc == 2) & (yp < y))
            side = jnp.where(zsrc == 3, 1, 0)
            copy = send(slot, xbuf.at[4 * side + y], xh_s.at[k, j], xh_r.at[side, j], at(x + 1, z, yp))
            pl.when(needed)(copy.start)
            sent.append((needed, copy))
        if k == 0:
            loads[0].wait()
            early = []
            for zp in range(Q):
                block = 16 * x + 4 * zp + y
                begin, first, last = jnp.int32(0), jnp.int32(0), jnp.int32(0)
                for k in range(docs.shape[0]):
                    end = begin + docs_v[k]
                    inside = (begin <= block) & (block < end)
                    first = jnp.where(inside, begin, first)
                    last = jnp.where(inside, end, last)
                    begin = end
                early.append([jnp.where(block - d >= first, 1.0, 0.0).astype(F32) for d in range(LAGS)])
                for d in range(LAGS):
                    late_m[zp, d] = jnp.where(block + d < last, 1.0, 0.0).astype(F32)

            row0 = lax.broadcasted_iota(jnp.int32, (T, C), 0) == 0
            loads[1].wait()
            loads[2].wait()
            for d in range(LAGS):
                tap = taps[d * T : (d + 1) * T, :]
                value = dot(tab[1], jnp.concatenate([tap, tap], axis=0))
                if d > 0:
                    before = taps[(d - 1) * T : d * T, :]
                    value += dot(tab[0], jnp.concatenate([before, before], axis=0))
                real, imag = value[:T], value[T:]
                kr[d] = real
                ki[d] = jnp.where(row0, 0.0, imag)
                kn[d] = jnp.where(row0, imag, real)
            for h, step in enumerate(steps):
                relays[h].wait_recv()
                half = xbuf.at[8 + 4 * lax.rem(z + 4 - step, Q) + y].at[halves[h]]
                copy = send(rbuf.at[h], half, zf_s.at[h], zf_r.at[h], at(x, z + step, y))
                copy.start()
                waits.append(copy)
        if k == 1:
            pl.semaphore_wait(inside_sem, 2)
            g_copies = along_z(gate_v, gbuf.at[z], ga_s, ga_r)
            c_copies = along_z(cot_v, cbuf.at[z], ca_s, ca_r)
            waits += list(g_copies.values()) + list(c_copies.values())
        if earlier is not None:
            arrivals(earlier)
            transform(0, xbuf, 8 + 4 * earlier, 4, spec)
        earlier = zsrc
    arrivals(earlier)
    transform(0, xbuf, 8 + 4 * earlier, 4, spec)
    for side in (0, 1):
        for j in range(Q):
            ysrc = lax.rem(y + 4 - j, Q)
            slot = xbuf.at[4 * side + ysrc]
            copy = send(slot, slot, xh_s.at[0, j], xh_r.at[side, j], at(x + 3, z, ysrc))
            if side:
                copy.wait_recv()
            else:
                pl.when(y < ysrc)(copy.wait_recv)
    transform(0, xbuf, 0, 8, spec)

    def forward_tile(f, _):
        re, im = tile(f)
        for zp in range(Q):
            acc_r = jnp.zeros((8, C), F32)
            acc_i = jnp.zeros((8, C), F32)
            for d in range(LAGS):
                r = 8 + 4 * zp + y - d
                live = early[zp][d]
                s_r, s_i = spec[r, re, :] * live, spec[r, im, :] * live
                acc_r += kr[d, re, :] * s_r - ki[d, re, :] * s_i
                acc_i += kn[d, re, :] * s_i + ki[d, re, :] * s_r
            prod[re, zp * C : (zp + 1) * C] = acc_r
            prod[im, zp * C : (zp + 1) * C] = acc_i
        return 0

    lax.fori_loop(0, T // 8, forward_tile, 0)
    conv = inverse(slice(T, 2 * T), prod[...])
    for copies in (g_copies, c_copies):
        for k in (1, 3, 2):
            copies[k].wait_recv()

    ones = jnp.ones((2 * C, C), BF16)
    lane = lax.broadcasted_iota(jnp.int32, (T, C), 1)
    sums = jnp.zeros((T, C), F32)
    for zp in range(Q):
        mixed = conv[:, zp * C : (zp + 1) * C] + skip_v[...] * xbuf[8 + 4 * zp + y].astype(F32)
        zval[zp] = mixed
        gated = gbuf[zp].astype(F32) * mixed
        for number, values in ((zp, gated * gated), (Q + zp, cbuf[zp].astype(F32) * gated)):
            high = values.astype(BF16)
            low = (values - high.astype(F32)).astype(BF16)
            sums = jnp.where(lane == number, dot(jnp.concatenate([high, low], axis=1), ones), sums)
    own_r[0] = sums.T[:8]
    copy = send(own_r.at[0], own_r.at[1], p_ss.at[0], p_rs.at[0], ring(0, 1))
    copy.start()
    copy.wait()
    own_r[2] = own_r[0] + own_r[1]
    n_copies = []
    for i, step in enumerate(near):
        copy = send(own_r.at[2], near_r.at[i], n_ss.at[i], n_rs.at[i], ring(step, 0))
        copy.start()
        n_copies.append(copy)
    for copy in n_copies[1:]:
        copy.wait_recv()
    total = own_r[2] + ((near_r[1] + near_r[2]) + (near_r[3] + near_r[4]))
    wide_s[...] = total
    w_copies = []
    for i, step in enumerate(wide):
        copy = send(wide_s, wide_r.at[i], w_ss.at[i], w_rs.at[i], ring(step, 0))
        copy.start()
        w_copies.append(copy)
    for copy in n_copies[:1] + w_copies:
        copy.wait_recv()
    waits += n_copies + w_copies
    mean = (total + (wide_r[0] + wide_r[1]) + near_r[0]) / (Q * C * 8)
    inv_rows = lax.rsqrt(mean[0:4] + EPSILON)
    fac_rows = mean[4:8] * inv_rows * inv_rows * inv_rows
    factors = jnp.concatenate([inv_rows, fac_rows], axis=0).T

    d_sent = []
    for zp in range(Q):
        inv = jnp.broadcast_to(factors[:, zp : zp + 1], (T, C))
        fac = jnp.broadcast_to(factors[:, 4 + zp : 5 + zp], (T, C))
        mixed = zval[zp]
        gate_f = gbuf[zp].astype(F32)
        gated = gate_f * mixed
        dgated = cbuf[zp].astype(F32) * inv - gated * fac
        out_s[zp] = (gated * inv).astype(BF16)
        ggate_s[zp] = (dgated * mixed).astype(BF16)
        dbuf[zp, y] = (dgated * gate_f).astype(BF16)
        slot = dbuf.at[zp, y]
        for j in (2, 1, 3, 0):
            yp = lax.rem(y + j, Q)
            if j:
                needed = (y > yp) if zp == 0 else None
                copy = send(slot, slot, df_s.at[zp, j - 1], df_r.at[zp, j - 1], at(x, z, yp))
                d_sent.append((needed, copy))
            if zp < 2:
                needed = (yp > y) if zp == 1 else None
                copy = send(slot, dbuf.at[4 + zp, y], dh_s.at[zp, j], dh_r.at[zp, j], at(x + 3, z, yp))
                d_sent.append((needed, copy))
        for needed, copy in d_sent[len(d_sent) - (7 if zp < 2 else 3) :]:
            if needed is None:
                copy.start()
            else:
                pl.when(needed)(copy.start)
    for needed, copy in d_sent:
        sent.append((needed, copy))

    own_d = jnp.concatenate([dbuf[zp, y] for zp in range(Q)], axis=1)
    own_spec = dot(tab[1], jnp.concatenate([own_d, own_d], axis=0))
    for zp in range(Q):
        dspec[4 * zp + y] = own_spec[:, zp * C : (zp + 1) * C]

    def filter_tile(f, _):
        re, im = tile(f)
        first = (lax.broadcasted_iota(jnp.int32, (8, C), 0) == 0) & (f == 0)
        sign = (1 - 2 * (lax.broadcasted_iota(jnp.int32, (8, C), 0) % 2)).astype(F32)
        mine = []
        for zp in range(Q):
            d_r, d_i = dspec[4 * zp + y, re, :], dspec[4 * zp + y, im, :]
            mine.append((d_r, jnp.where(first, 0.0, d_i), jnp.where(first, -d_i, d_r)))
        prior = None
        for d in range(LAGS):
            acc_r = jnp.zeros((8, C), F32)
            acc_i = jnp.zeros((8, C), F32)
            for zp in range(Q):
                r = 8 + 4 * zp + y - d
                live = early[zp][d]
                s_r, s_i = spec[r, re, :] * live, spec[r, im, :] * live
                d_r, d_i, d_n = mine[zp]
                acc_r += d_r * s_r + d_i * s_i
                acc_i += d_i * s_r - d_n * s_i
            if prior is not None:
                cols = slice((d - 1) * C, d * C)
                gprod[re, cols] = prior[0] * sign + acc_r
                gprod[im, cols] = prior[1] * sign + acc_i
            prior = (acc_r, acc_i)
        cols = slice((LAGS - 1) * C, LAGS * C)
        gprod[re, cols] = prior[0] * sign
        gprod[im, cols] = prior[1] * sign
        return 0

    lax.fori_loop(0, T // 8, filter_tile, 0)
    scale = float(64 * T) ** (-0.5)
    for d in range(LAGS):
        value = inverse(slice(0, T), gprod[:, d * C : (d + 1) * C]) * scale
        for i in range(8):
            gf_s[d // 2, (i % 4) * 4 + 2 * (d % 2) + i // 4] = value[16 * i : 16 * i + 16].astype(BF16)
    gx_copies = []
    for k in (2, 1, 3):
        copy = send(gf_s.at[lax.rem(x + k, Q)], gf_r.at[k - 1], gx_ss.at[k - 1], gx_rs.at[k - 1], at(x + k, z, y))
        copy.start()
        gx_copies.append(copy)
    waits += gx_copies
    o_copies = back_along_z(out_s, out, ob_s, ob_r)
    gg_copies = back_along_z(ggate_s, ggate, gb_s, gb_r)

    def spectra(blocks, slots):
        wide_d = jnp.concatenate(blocks, axis=1)
        value = dot(tab[1], jnp.concatenate([wide_d, wide_d], axis=0))
        for k, slot in enumerate(slots):
            dspec[slot] = value[:, k * C : (k + 1) * C]

    for j in (1, 3, 2):
        ysrc = lax.rem(y + 4 - j, Q)
        for zp in range(Q):
            slot = dbuf.at[zp, ysrc]
            copy = send(slot, slot, df_s.at[zp, j - 1], df_r.at[zp, j - 1], at(x, z, ysrc))
            if zp == 0:
                pl.when(ysrc > y)(copy.wait_recv)
            else:
                copy.wait_recv()
        spectra([dbuf[zp, ysrc] for zp in range(Q)], [4 * zp + ysrc for zp in range(Q)])
    for j in (0, 1, 3, 2):
        ysrc = lax.rem(y + 4 - j, Q)
        for zp in range(2):
            slot = dbuf.at[4 + zp, ysrc]
            copy = send(slot, slot, dh_s.at[zp, j], dh_r.at[zp, j], at(x + 1, z, ysrc))
            if zp == 1:
                pl.when(y > ysrc)(copy.wait_recv)
            else:
                copy.wait_recv()
        spectra([dbuf[4 + zp, ysrc] for zp in range(2)], [16 + 4 * zp + ysrc for zp in range(2)])

    s_copies = {}
    for k in (2, 1, 3, 0):
        zp = lax.rem(z + k, Q)

        def backward_tile(f, _):
            re, im = tile(f)
            acc_r = jnp.zeros((8, C), F32)
            acc_i = jnp.zeros((8, C), F32)
            for d in range(LAGS):
                r = 4 * zp + y + d
                live = late_m[zp, d]
                s_r, s_i = dspec[r, re, :] * live, dspec[r, im, :] * live
                acc_r += kr[d, re, :] * s_r + ki[d, re, :] * s_i
                acc_i += kn[d, re, :] * s_i - ki[d, re, :] * s_r
            prod[re, :C] = acc_r
            prod[im, :C] = acc_i
            return 0

        lax.fori_loop(0, T // 8, backward_tile, 0)
        conv = inverse(slice(0, T), prod[:, :C])
        gsig_s[zp] = (conv + skip_v[...] * dbuf[zp, y].astype(F32)).astype(BF16)
        if k:
            s_copies[k] = send(gsig_s.at[zp], gsig.at[:, lanes], sb_s.at[k - 1], sb_r.at[k - 1], at(x, zp, y))
            s_copies[k].start()
    gsig[:, lanes] = gsig_s[z]

    for copy in gx_copies:
        copy.wait_recv()
    gy_s[...] = (
        gf_s[x].astype(F32) + gf_r[0].astype(F32) + gf_r[1].astype(F32) + gf_r[2].astype(F32)
    ).reshape(Q, 4, 16, C)
    gy_copies = []
    for k in (2, 1, 3):
        copy = send(gy_s.at[lax.rem(y + k, Q)], gy_r.at[k - 1], gy_ss.at[k - 1], gy_rs.at[k - 1], at(x, z, y + k))
        copy.start()
        gy_copies.append(copy)
    waits += gy_copies

    for copy in gy_copies:
        copy.wait_recv()
    gz_s[...] = gy_s[y] + gy_r[0] + gy_r[1] + gy_r[2]
    gz_copies = back_along_z(gz_s, gfilt, gz_ss, gz_rs)

    for copies in (o_copies, gg_copies, s_copies, gz_copies):
        for copy in copies.values():
            copy.wait()
    for copy in waits:
        copy.wait_send()
    for needed, copy in sent:
        if needed is None:
            copy.wait_send()
        else:
            pl.when(needed)(copy.wait_send)


def finish(a, b, c, d, e, f, g, h, sems):
    copies = [pltpu.make_async_copy(s, t, sems.at[i]) for i, (s, t) in enumerate(((a, e), (b, f), (c, g), (d, h)))]
    for copy in copies:
        copy.start()
    for copy in copies:
        copy.wait()


def on_device(signal, gate_input, filters, skip_weight, doc_lengths, grad_out):
    channels = signal.shape[1]
    vmem, hbm = pl.BlockSpec(memory_space=pltpu.VMEM), pl.BlockSpec(memory_space=pltpu.HBM)
    dma = lambda *shape: pltpu.SemaphoreType.DMA(shape)
    block = (T, channels)
    three = [dma(3)] * 2
    scratch = [
        pltpu.SMEM(doc_lengths.shape, jnp.int32), pltpu.SMEM((Q, LAGS), F32),
        pltpu.VMEM((1, C), F32),
        pltpu.VMEM(block, BF16), pltpu.VMEM(block, BF16), pltpu.VMEM(block, BF16),
        pltpu.VMEM((LAGS * T, C), BF16), pltpu.VMEM((4, 2 * T, 2 * T), BF16),
        pltpu.VMEM((24, T, C), BF16), pltpu.VMEM((Q, T, C), BF16), pltpu.VMEM((Q, T, C), BF16),
        pltpu.VMEM((6, Q, T, C), BF16), pltpu.VMEM((2, T // 2, C), BF16),
        pltpu.VMEM((24, 2 * T, C), F32), pltpu.VMEM((24, 2 * T, C), F32),
        pltpu.VMEM((LAGS, T, C), F32), pltpu.VMEM((LAGS, T, C), F32), pltpu.VMEM((LAGS, T, C), F32),
        pltpu.VMEM((2 * T, Q * C), F32), pltpu.VMEM((2 * T, LAGS * C), F32), pltpu.VMEM((Q, T, C), F32),
        pltpu.VMEM((Q, T, C), BF16), pltpu.VMEM((Q, T, C), BF16), pltpu.VMEM((Q, T, C), BF16),
        pltpu.VMEM((3, 8, T), F32), pltpu.VMEM((5, 8, T), F32),
        pltpu.VMEM((8, T), F32), pltpu.VMEM((2, 8, T), F32),
        pltpu.VMEM((Q, 16, 16, C), BF16), pltpu.VMEM((3, 16, 16, C), BF16),
        pltpu.VMEM((Q, 4, 16, C), F32), pltpu.VMEM((3, 4, 16, C), F32), pltpu.VMEM((4, 16, C), F32),
        pltpu.SemaphoreType.REGULAR, dma(10), *three, dma(2), dma(2), dma(2), dma(2), *three, *three, dma(4, 3), dma(4, 3), dma(4, 4), dma(2, 4), dma(1), dma(1), dma(5), dma(5), dma(2), dma(2),
        dma(4, 3), dma(4, 3), dma(2, 4), dma(2, 4), *three, *three, *three, *three, *three, *three,
    ]
    shapes = (
        jax.ShapeDtypeStruct(block, BF16), jax.ShapeDtypeStruct(block, BF16),
        jax.ShapeDtypeStruct(block, BF16), jax.ShapeDtypeStruct((16, channels), F32),
    )
    results = pl.pallas_call(
        kernel,
        out_shape=shapes,
        in_specs=[hbm] * 7,
        out_specs=(vmem,) * 4,
        scratch_shapes=scratch,
        compiler_params=pltpu.CompilerParams(
            collective_id=0, has_side_effects=True, vmem_limit_bytes=63 << 20
        ),
        name="hyena",
    )(doc_lengths, skip_weight[None, :], signal, gate_input, filters, grad_out, jnp.asarray(tables()))
    return pl.pallas_call(
        finish,
        out_shape=shapes,
        in_specs=[vmem] * 4,
        out_specs=(hbm,) * 4,
        scratch_shapes=[dma(4)],
        name="finish",
    )(*results)


def solution(mesh):
    placed = (P("seq", "tp"), P("seq", "tp"), P(None, "tp"), P("tp"), P(), P("seq", "tp"))
    return jax.shard_map(
        on_device,
        mesh=mesh,
        in_specs=placed,
        out_specs=(P("seq", "tp"), P("seq", "tp"), P("seq", "tp"), P("seq", "tp")),
        check_vma=False,
    )
```

time: 93.7 us -> 76.5 us (0.82)
  the two profiles are of different devices: /device:TPU:8 before, /device:TPU:2 now
where the time goes in v2:
time: 76.5 us; the launch traced here: 76.4 us
  Pallas kernels  75.7 us (99%)
    pallas_call x1, Pallas kernels, on_device(): pl.pallas_call(kernel, out_shape=shapes, in_specs=[hbm] * 7, out_specs=(v...  73.9 us
    pallas_call x1, Pallas kernels, on_device(): pl.pallas_call(finish, out_shape=shapes, in_specs=[vmem] * 4, out_specs=(...  1.81 us

profile of v2, /device:TPU:2, one launch (start us, length us, event | category | flops | bytes accessed | tf_op | source)
XLA Modules:
  0.0 76.4 jit_solution(1309828491792962064)
XLA Ops:
  0.6 73.9 %hyena.1 = (bf16[128,512]{1,0:T(8,128)(2,1)}, bf16[128,512]{1,0:T(8,128)(2,1)}, bf16[128,512]{1,0:T(8,128)(2,1)}, f32[16,512]{1,0:T(8,128)}) custom-call(s32[16]{0:T(128)} %docs.1, f32[1,512]{1,0:T(1,128)} %bitcast.1, bf16[128,512]{1,0:T(8,128)(2,1)} %signal.1, bf16[128,512]{1,0:T(8,128)(2,1)} %gate.1, bf16[1024,512]{1,0:T(8,128)(2,1)} %filters.1, ...), custom_call_target="tpu_custom_call" | custom-call | tf_op jit(solution)/shard_map/hyena/pallas_call | solution.py:507
  74.6 1.8 %finish.1 = (bf16[128,512]{1,0:T(8,128)(2,1)}, bf16[128,512]{1,0:T(8,128)(2,1)}, bf16[128,512]{1,0:T(8,128)(2,1)}, f32[16,512]{1,0:T(8,128)}) custom-call(bf16[128,512]{1,0:T(8,128)(2,1)} %get-tuple-element.8.a, bf16[128,512]{1,0:T(8,128)(2,1)} %get-tuple-element.9.b, bf16[128,512]{1,0:T(8,128)(2,1)} %get-tuple-element.10.c, f32[16,512]{1,0:T(8,128)} %get-tuple-element.11.d), custom_call_target="tpu_custom_call" | custom-call | tf_op jit(solution)/shard_map/finish/pallas_call | solution.py:518

commit v3 on v2

--- a/solution.py
+++ b/solution.py
@@ -52,10 +52,10 @@
     docs, skip, signal, gate, filters, cotangent, table,
     out, gsig, ggate, gfilt,
     docs_v, late_m, skip_v, sig_v, gate_v, cot_v, taps, tab, xbuf, gbuf, cbuf, dbuf, rbuf, spec, dspec, kr, ki, kn,
-    prod, gprod, zval, out_s, ggate_s, gsig_s, own_r, near_r, wide_s, wide_r,
-    gf_s, gf_r, gy_s, gy_r, gz_s,
-    inside_sem, load_sem, za_s, za_r, zr_s, zr_r, zf_s, zf_r, ga_s, ga_r, ca_s, ca_r, yf_s, yf_r, xh_s, xh_r, p_ss, p_rs, n_ss, n_rs, w_ss, w_rs,
-    df_s, df_r, dh_s, dh_r, ob_s, ob_r, gb_s, gb_r, sb_s, sb_r, gx_ss, gx_rs, gy_ss, gy_rs, gz_ss, gz_rs,
+    prod, gprod, zval, inv_b, fac_b, z_s, z_r, gsig_s, own_r, near_r, far_r, wide_s, wide_r,
+    gf_s, gf_r, gz_s,
+    inside_sem, load_sem, za_s, za_r, zr_s, zr_r, zf_s, zf_r, ga_s, ga_r, ca_s, ca_r, yf_s, yf_r, xh_s, xh_r, n_ss, n_rs, w_ss, w_rs,
+    df_s, df_r, dh_s, dh_r, zb_s, zb_r, sb_s, sb_r, gx_ss, gx_rs, gz_ss, gz_rs,
 ):
     seq, tpi = lax.axis_index("seq"), lax.axis_index("tp")
     x, z, y = seq // 16, (seq // 4) % 4, seq % 4
@@ -77,9 +77,9 @@
         spot = lax.rem(place + step + 16, 16)
         return (16 * x + 4 * (spot // 4) + y, 2 * lax.rem(spot, 4) + lax.rem(core + other, 2))
 
-    near = (8, 2, -2, 1, -1)
+    near = [(8, 0), (8, 1)] + [(step, other) for step in (2, -2, 1, -1) for other in (0, 1)] + [(0, 1)]
     wide = (5, -5)
-    partners += [ring(step, 0) for step in near[1:]] + [ring(0, 1)]
+    partners += [ring(step, other) for step, other in near[2:]]
     for partner in partners:
         pl.semaphore_signal(barrier, inc=1, device_id=partner, device_id_type=MESH)
 
@@ -169,7 +169,6 @@
             copy = send(slot, slot, yf_s.at[0, j - 1], yf_r.at[zsrc, j - 1], at(x, z, ysrc))
             pl.when((zsrc < 3) | (y > ysrc))(copy.wait_recv)
 
-    earlier = None
     for k in (0, 1, 3, 2):
         zsrc = lax.rem(z + 4 - k, Q)
         slot = xbuf.at[8 + 4 * zsrc + y]
@@ -179,19 +178,32 @@
                 send(half, half, zf_s.at[h], zf_r.at[h], at(x, z + 2, y)).wait_recv()
         elif k:
             send(slot, slot, za_s.at[k - 1], za_r.at[k - 1], at(x, z + k, y)).wait_recv()
-        for j in (2, 1, 3, 0):
+        side = jnp.where(zsrc == 3, 1, 0)
+        ways = [("y", j) for j in (2, 1, 3)]
+        halo = [("x", j) for j in (2, 1, 3, 0)]
+        for way, j in halo + ways if k == 2 else ways + halo:
             yp = lax.rem(y + j, Q)
-            if j:
+            if way == "y":
                 needed = (zsrc < 3) | (yp > y)
                 copy = send(slot, slot, yf_s.at[k, j - 1], yf_r.at[zsrc, j - 1], at(x, z, yp))
-                pl.when(needed)(copy.start)
-                sent.append((needed, copy))
-            needed = (zsrc == 3) | ((zsrc == 2) & (yp < y))
-            side = jnp.where(zsrc == 3, 1, 0)
-            copy = send(slot, xbuf.at[4 * side + y], xh_s.at[k, j], xh_r.at[side, j], at(x + 1, z, yp))
+            else:
+                needed = (zsrc == 3) | ((zsrc == 2) & (yp < y))
+                copy = send(slot, xbuf.at[4 * side + y], xh_s.at[k, j], xh_r.at[side, j], at(x + 1, z, yp))
             pl.when(needed)(copy.start)
             sent.append((needed, copy))
         if k == 0:
+            for h, step in enumerate(steps):
+                relays[h].wait_recv()
+                half = xbuf.at[8 + 4 * lax.rem(z + 4 - step, Q) + y].at[halves[h]]
+                copy = send(rbuf.at[h], half, zf_s.at[h], zf_r.at[h], at(x, z + step, y))
+                copy.start()
+                waits.append(copy)
+        if k == 1:
+            pl.semaphore_wait(inside_sem, 2)
+            g_copies = along_z(gate_v, gbuf.at[z], ga_s, ga_r)
+            c_copies = along_z(cot_v, cbuf.at[z], ca_s, ca_r)
+            waits += list(g_copies.values()) + list(c_copies.values())
+        if k == 3:
             loads[0].wait()
             early = []
             for zp in range(Q):
@@ -220,23 +232,12 @@
                 kr[d] = real
                 ki[d] = jnp.where(row0, 0.0, imag)
                 kn[d] = jnp.where(row0, imag, real)
-            for h, step in enumerate(steps):
-                relays[h].wait_recv()
-                half = xbuf.at[8 + 4 * lax.rem(z + 4 - step, Q) + y].at[halves[h]]
-                copy = send(rbuf.at[h], half, zf_s.at[h], zf_r.at[h], at(x, z + step, y))
-                copy.start()
-                waits.append(copy)
-        if k == 1:
-            pl.semaphore_wait(inside_sem, 2)
-            g_copies = along_z(gate_v, gbuf.at[z], ga_s, ga_r)
-            c_copies = along_z(cot_v, cbuf.at[z], ca_s, ca_r)
-            waits += list(g_copies.values()) + list(c_copies.values())
-        if earlier is not None:
-            arrivals(earlier)
-            transform(0, xbuf, 8 + 4 * earlier, 4, spec)
-        earlier = zsrc
-    arrivals(earlier)
-    transform(0, xbuf, 8 + 4 * earlier, 4, spec)
+            for step in (0, 1, 3):
+                earlier = lax.rem(z + 4 - step, Q)
+                arrivals(earlier)
+                transform(0, xbuf, 8 + 4 * earlier, 4, spec)
+    arrivals(zsrc)
+    transform(0, xbuf, 8 + 4 * zsrc, 4, spec)
     for side in (0, 1):
         for j in range(Q):
             ysrc = lax.rem(y + 4 - j, Q)
@@ -275,67 +276,84 @@
     for zp in range(Q):
         mixed = conv[:, zp * C : (zp + 1) * C] + skip_v[...] * xbuf[8 + 4 * zp + y].astype(F32)
         zval[zp] = mixed
+        z_s[zp, 0] = mixed.astype(BF16)
+        z_s[zp, 1] = (mixed - mixed.astype(BF16).astype(F32)).astype(BF16)
         gated = gbuf[zp].astype(F32) * mixed
         for number, values in ((zp, gated * gated), (Q + zp, cbuf[zp].astype(F32) * gated)):
             high = values.astype(BF16)
             low = (values - high.astype(F32)).astype(BF16)
             sums = jnp.where(lane == number, dot(jnp.concatenate([high, low], axis=1), ones), sums)
-    own_r[0] = sums.T[:8]
-    copy = send(own_r.at[0], own_r.at[1], p_ss.at[0], p_rs.at[0], ring(0, 1))
-    copy.start()
-    copy.wait()
-    own_r[2] = own_r[0] + own_r[1]
+    own_r[...] = sums.T[:8]
     n_copies = []
-    for i, step in enumerate(near):
-        copy = send(own_r.at[2], near_r.at[i], n_ss.at[i], n_rs.at[i], ring(step, 0))
+    for i, (step, other) in enumerate(near):
+        dst = far_r.at[i] if i < 2 else near_r.at[i - 2]
+        copy = send(own_r, dst, n_ss.at[i], n_rs.at[i], ring(step, other))
         copy.start()
         n_copies.append(copy)
-    for copy in n_copies[1:]:
+    for copy in n_copies[2:]:
         copy.wait_recv()
-    total = own_r[2] + ((near_r[1] + near_r[2]) + (near_r[3] + near_r[4]))
+    total = own_r[...]
+    for i in range(9):
+        total += near_r[i]
     wide_s[...] = total
     w_copies = []
     for i, step in enumerate(wide):
         copy = send(wide_s, wide_r.at[i], w_ss.at[i], w_rs.at[i], ring(step, 0))
         copy.start()
         w_copies.append(copy)
-    for copy in n_copies[:1] + w_copies:
+    zb_copies = []
+    for k in (2, 1, 3):
+        copy = send(z_s.at[lax.rem(z + k, Q)], z_r.at[z], zb_s.at[k - 1], zb_r.at[k - 1], at(x, z + k, y))
+        copy.start()
+        zb_copies.append(copy)
+    for copy in n_copies[:2] + w_copies:
         copy.wait_recv()
     waits += n_copies + w_copies
-    mean = (total + (wide_r[0] + wide_r[1]) + near_r[0]) / (Q * C * 8)
+    mean = (total + (wide_r[0] + wide_r[1]) + (far_r[0] + far_r[1])) / (Q * C * 8)
     inv_rows = lax.rsqrt(mean[0:4] + EPSILON)
     fac_rows = mean[4:8] * inv_rows * inv_rows * inv_rows
     factors = jnp.concatenate([inv_rows, fac_rows], axis=0).T
 
-    d_sent = []
     for zp in range(Q):
         inv = jnp.broadcast_to(factors[:, zp : zp + 1], (T, C))
         fac = jnp.broadcast_to(factors[:, 4 + zp : 5 + zp], (T, C))
-        mixed = zval[zp]
+        inv_b[zp] = inv
+        fac_b[zp] = fac
         gate_f = gbuf[zp].astype(F32)
-        gated = gate_f * mixed
-        dgated = cbuf[zp].astype(F32) * inv - gated * fac
-        out_s[zp] = (gated * inv).astype(BF16)
-        ggate_s[zp] = (dgated * mixed).astype(BF16)
+        dgated = cbuf[zp].astype(F32) * inv - gate_f * zval[zp] * fac
         dbuf[zp, y] = (dgated * gate_f).astype(BF16)
-        slot = dbuf.at[zp, y]
+
+    def by_z(*values):
+        result = jnp.int32(values[0])
+        for number in range(1, Q):
+            result = jnp.where(z == number, values[number], result)
+        return result
+
+    quads = [by_z(*row) for row in ((2, 3, 0, 1), (3, 4, 1, 2), (4, 5, 2, 3), (1, 2, 3, 0), (5, 0, 4, 4), (0, 1, 5, 5))]
+    order = [by_z(*row) for row in ((2, 3, 0, 1), (1, 2, 1, 0), (3, 0, 3, 2), (0, 1, 2, 3))]
+
+    def quad_copies(quad, way):
+        result = []
         for j in (2, 1, 3, 0):
-            yp = lax.rem(y + j, Q)
+            other = lax.rem(y + Q + way * j, Q)
+            source, target = (y, other) if way == 1 else (other, y)
             if j:
-                needed = (y > yp) if zp == 0 else None
-                copy = send(slot, slot, df_s.at[zp, j - 1], df_r.at[zp, j - 1], at(x, z, yp))
-                d_sent.append((needed, copy))
-            if zp < 2:
-                needed = (yp > y) if zp == 1 else None
-                copy = send(slot, dbuf.at[4 + zp, y], dh_s.at[zp, j], dh_r.at[zp, j], at(x + 3, z, yp))
-                d_sent.append((needed, copy))
-        for needed, copy in d_sent[len(d_sent) - (7 if zp < 2 else 3) :]:
-            if needed is None:
-                copy.start()
-            else:
-                pl.when(needed)(copy.start)
-    for needed, copy in d_sent:
-        sent.append((needed, copy))
+                own_quad = lax.rem(quad, Q)
+                slot = dbuf.at[own_quad, source]
+                copy = send(slot, slot, df_s.at[own_quad, j - 1], df_r.at[own_quad, j - 1], at(x, z, other))
+                result.append(((quad < Q) & ((quad > 0) | (source > target)), copy))
+            side = lax.rem(quad, 2)
+            copy = send(
+                dbuf.at[side, source], dbuf.at[4 + side, source], dh_s.at[side, j], dh_r.at[side, j],
+                at(x + (3 if way == 1 else 1), z, other),
+            )
+            result.append(((quad == 4) | ((quad == 5) & (target > source)), copy))
+        return result
+
+    for quad in quads:
+        for needed, copy in quad_copies(quad, 1):
+            pl.when(needed)(copy.start)
+            sent.append((needed, copy))
 
     own_d = jnp.concatenate([dbuf[zp, y] for zp in range(Q)], axis=1)
     own_spec = dot(tab[1], jnp.concatenate([own_d, own_d], axis=0))
@@ -373,50 +391,31 @@
 
     lax.fori_loop(0, T // 8, filter_tile, 0)
     scale = float(64 * T) ** (-0.5)
-    for d in range(LAGS):
-        value = inverse(slice(0, T), gprod[:, d * C : (d + 1) * C]) * scale
-        for i in range(8):
-            gf_s[d // 2, (i % 4) * 4 + 2 * (d % 2) + i // 4] = value[16 * i : 16 * i + 16].astype(BF16)
+    for half in range(Q):
+        value = inverse(slice(0, T), gprod[:, 2 * half * C : 2 * (half + 1) * C]) * scale
+        for odd in range(2):
+            for i in range(8):
+                piece = value[16 * i : 16 * i + 16, odd * C : (odd + 1) * C].astype(BF16)
+                gf_s[half, i % 4, 2 * odd + i // 4] = piece
     gx_copies = []
-    for k in (2, 1, 3):
-        copy = send(gf_s.at[lax.rem(x + k, Q)], gf_r.at[k - 1], gx_ss.at[k - 1], gx_rs.at[k - 1], at(x + k, z, y))
+    around = [(i, k) for i in (2, 1, 3, 0) for k in (2, 1, 3, 0) if i or k]
+    for n, (i, k) in enumerate(around):
+        copy = send(
+            gf_s.at[lax.rem(x + i, Q), lax.rem(y + k, Q)], gf_r.at[n], gx_ss.at[n], gx_rs.at[n], at(x + i, z, y + k)
+        )
         copy.start()
         gx_copies.append(copy)
     waits += gx_copies
-    o_copies = back_along_z(out_s, out, ob_s, ob_r)
-    gg_copies = back_along_z(ggate_s, ggate, gb_s, gb_r)
-
-    def spectra(blocks, slots):
-        wide_d = jnp.concatenate(blocks, axis=1)
-        value = dot(tab[1], jnp.concatenate([wide_d, wide_d], axis=0))
-        for k, slot in enumerate(slots):
-            dspec[slot] = value[:, k * C : (k + 1) * C]
-
-    for j in (1, 3, 2):
-        ysrc = lax.rem(y + 4 - j, Q)
-        for zp in range(Q):
-            slot = dbuf.at[zp, ysrc]
-            copy = send(slot, slot, df_s.at[zp, j - 1], df_r.at[zp, j - 1], at(x, z, ysrc))
-            if zp == 0:
-                pl.when(ysrc > y)(copy.wait_recv)
-            else:
-                copy.wait_recv()
-        spectra([dbuf[zp, ysrc] for zp in range(Q)], [4 * zp + ysrc for zp in range(Q)])
-    for j in (0, 1, 3, 2):
-        ysrc = lax.rem(y + 4 - j, Q)
-        for zp in range(2):
-            slot = dbuf.at[4 + zp, ysrc]
-            copy = send(slot, slot, dh_s.at[zp, j], dh_r.at[zp, j], at(x + 1, z, ysrc))
-            if zp == 1:
-                pl.when(y > ysrc)(copy.wait_recv)
-            else:
-                copy.wait_recv()
-        spectra([dbuf[4 + zp, ysrc] for zp in range(2)], [16 + 4 * zp + ysrc for zp in range(2)])
-
-    s_copies = {}
-    for k in (2, 1, 3, 0):
-        zp = lax.rem(z + k, Q)
-
+
+    def arrive(quad):
+        for needed, copy in quad_copies(quad, -1):
+            pl.when(needed)(copy.wait_recv)
+        blocks = jnp.concatenate([dbuf[quad, k] for k in range(Q)], axis=1)
+        value = dot(tab[1], jnp.concatenate([blocks, blocks], axis=0))
+        for k in range(Q):
+            dspec[4 * quad + k] = value[:, k * C : (k + 1) * C]
+
+    def signal_gradient(zp):
         def backward_tile(f, _):
             re, im = tile(f)
             acc_r = jnp.zeros((8, C), F32)
@@ -434,31 +433,53 @@
         lax.fori_loop(0, T // 8, backward_tile, 0)
         conv = inverse(slice(0, T), prod[:, :C])
         gsig_s[zp] = (conv + skip_v[...] * dbuf[zp, y].astype(F32)).astype(BF16)
-        if k:
-            s_copies[k] = send(gsig_s.at[zp], gsig.at[:, lanes], sb_s.at[k - 1], sb_r.at[k - 1], at(x, zp, y))
-            s_copies[k].start()
-    gsig[:, lanes] = gsig_s[z]
+
+    s_copies = []
+
+    def give(number):
+        zp = order[number]
+        step = lax.rem(zp + Q - z, Q) - 1
+        signal_gradient(zp)
+        copy = send(gsig_s.at[zp], gsig.at[:, lanes], sb_s.at[step], sb_r.at[step], at(x, zp, y))
+        copy.start()
+        s_copies.append(copy)
+
+    for quad in quads[:3]:
+        arrive(quad)
+    give(0)
+    arrive(quads[3])
+    give(1)
+
+    arrive(quads[4])
+    arrive(quads[5])
+    give(2)
 
     for copy in gx_copies:
         copy.wait_recv()
-    gy_s[...] = (
-        gf_s[x].astype(F32) + gf_r[0].astype(F32) + gf_r[1].astype(F32) + gf_r[2].astype(F32)
-    ).reshape(Q, 4, 16, C)
-    gy_copies = []
-    for k in (2, 1, 3):
-        copy = send(gy_s.at[lax.rem(y + k, Q)], gy_r.at[k - 1], gy_ss.at[k - 1], gy_rs.at[k - 1], at(x, z, y + k))
-        copy.start()
-        gy_copies.append(copy)
-    waits += gy_copies
-
-    for copy in gy_copies:
-        copy.wait_recv()
-    gz_s[...] = gy_s[y] + gy_r[0] + gy_r[1] + gy_r[2]
+    total = gf_s[x, y].astype(F32)
+    for n in range(len(around)):
+        total += gf_r[n].astype(F32)
+    gz_s[...] = total
     gz_copies = back_along_z(gz_s, gfilt, gz_ss, gz_rs)
-
-    for copies in (o_copies, gg_copies, s_copies, gz_copies):
-        for copy in copies.values():
-            copy.wait()
+    signal_gradient(z)
+    gsig[:, lanes] = gsig_s[z]
+
+    z_r[z] = z_s[z]
+    for copy in zb_copies:
+        copy.wait()
+    inv, fac = inv_b[z], fac_b[z]
+    for j in range(Q):
+        cols = slice(j * C, (j + 1) * C)
+        mixed = z_r[j, 0].astype(F32) + z_r[j, 1].astype(F32)
+        gated = gate_v[:, cols].astype(F32) * mixed
+        dgated = cot_v[:, cols].astype(F32) * inv - gated * fac
+        out[:, cols] = (gated * inv).astype(BF16)
+        ggate[:, cols] = (dgated * mixed).astype(BF16)
+
+    for copy in s_copies:
+        copy.wait()
+    for copy in gz_copies.values():
+        copy.wait()
     for copy in waits:
         copy.wait_send()
     for needed, copy in sent:
@@ -492,13 +513,13 @@
         pltpu.VMEM((24, 2 * T, C), F32), pltpu.VMEM((24, 2 * T, C), F32),
         pltpu.VMEM((LAGS, T, C), F32), pltpu.VMEM((LAGS, T, C), F32), pltpu.VMEM((LAGS, T, C), F32),
         pltpu.VMEM((2 * T, Q * C), F32), pltpu.VMEM((2 * T, LAGS * C), F32), pltpu.VMEM((Q, T, C), F32),
-        pltpu.VMEM((Q, T, C), BF16), pltpu.VMEM((Q, T, C), BF16), pltpu.VMEM((Q, T, C), BF16),
-        pltpu.VMEM((3, 8, T), F32), pltpu.VMEM((5, 8, T), F32),
+        pltpu.VMEM((Q, T, C), F32), pltpu.VMEM((Q, T, C), F32),
+        pltpu.VMEM((Q, 2, T, C), BF16), pltpu.VMEM((Q, 2, T, C), BF16), pltpu.VMEM((Q, T, C), BF16),
+        pltpu.VMEM((8, T), F32), pltpu.VMEM((9, 8, T), F32), pltpu.VMEM((2, 8, T), F32),
         pltpu.VMEM((8, T), F32), pltpu.VMEM((2, 8, T), F32),
-        pltpu.VMEM((Q, 16, 16, C), BF16), pltpu.VMEM((3, 16, 16, C), BF16),
-        pltpu.VMEM((Q, 4, 16, C), F32), pltpu.VMEM((3, 4, 16, C), F32), pltpu.VMEM((4, 16, C), F32),
-        pltpu.SemaphoreType.REGULAR, dma(10), *three, dma(2), dma(2), dma(2), dma(2), *three, *three, dma(4, 3), dma(4, 3), dma(4, 4), dma(2, 4), dma(1), dma(1), dma(5), dma(5), dma(2), dma(2),
-        dma(4, 3), dma(4, 3), dma(2, 4), dma(2, 4), *three, *three, *three, *three, *three, *three,
+        pltpu.VMEM((Q, Q, 4, 16, C), BF16), pltpu.VMEM((15, 4, 16, C), BF16), pltpu.VMEM((4, 16, C), F32),
+        pltpu.SemaphoreType.REGULAR, dma(10), *three, dma(2), dma(2), dma(2), dma(2), *three, *three, dma(4, 3), dma(4, 3), dma(4, 4), dma(2, 4), dma(11), dma(11), dma(2), dma(2),
+        dma(4, 3), dma(4, 3), dma(2, 4), dma(2, 4), *three, *three, dma(15), dma(15), *three,
     ]
     shapes = (
         jax.ShapeDtypeStruct(block, BF16), jax.ShapeDtypeStruct(block, BF16),

time: 76.5 us -> 72.8 us (0.952)
  the two profiles are of different devices: /device:TPU:2 before, /device:TPU:8 now
where the time goes in v3:
time: 72.8 us; the launch traced here: 72.6 us
  Pallas kernels  72 us (99%)
    pallas_call x1, Pallas kernels, on_device(): pl.pallas_call(kernel, out_shape=shapes, in_specs=[hbm] * 7, out_specs=(v...  70.2 us
    pallas_call x1, Pallas kernels, on_device(): pl.pallas_call(finish, out_shape=shapes, in_specs=[vmem] * 4, out_specs=(...  1.81 us

profile of v3, /device:TPU:8, one launch (start us, length us, event | category | flops | bytes accessed | tf_op | source)
XLA Modules:
  0.0 72.6 jit_solution(15140886130025562508)
XLA Ops:
  0.6 70.2 %hyena.1 = (bf16[128,512]{1,0:T(8,128)(2,1)}, bf16[128,512]{1,0:T(8,128)(2,1)}, bf16[128,512]{1,0:T(8,128)(2,1)}, f32[16,512]{1,0:T(8,128)}) custom-call(s32[16]{0:T(128)} %docs.1, f32[1,512]{1,0:T(1,128)} %bitcast.1, bf16[128,512]{1,0:T(8,128)(2,1)} %signal.1, bf16[128,512]{1,0:T(8,128)(2,1)} %gate.1, bf16[1024,512]{1,0:T(8,128)(2,1)} %filters.1, ...), custom_call_target="tpu_custom_call" | custom-call | tf_op jit(solution)/shard_map/hyena/pallas_call | solution.py:528
  70.8 1.8 %finish.1 = (bf16[128,512]{1,0:T(8,128)(2,1)}, bf16[128,512]{1,0:T(8,128)(2,1)}, bf16[128,512]{1,0:T(8,128)(2,1)}, f32[16,512]{1,0:T(8,128)}) custom-call(bf16[128,512]{1,0:T(8,128)(2,1)} %get-tuple-element.8.a, bf16[128,512]{1,0:T(8,128)(2,1)} %get-tuple-element.9.b, bf16[128,512]{1,0:T(8,128)(2,1)} %get-tuple-element.10.c, f32[16,512]{1,0:T(8,128)} %get-tuple-element.11.d), custom_call_target="tpu_custom_call" | custom-call | tf_op jit(solution)/shard_map/finish/pallas_call | solution.py:539

commit v4 on v3

--- a/solution.py
+++ b/solution.py
@@ -52,9 +52,9 @@
     docs, skip, signal, gate, filters, cotangent, table,
     out, gsig, ggate, gfilt,
     docs_v, late_m, skip_v, sig_v, gate_v, cot_v, taps, tab, xbuf, gbuf, cbuf, dbuf, rbuf, spec, dspec, kr, ki, kn,
-    prod, gprod, zval, inv_b, fac_b, z_s, z_r, gsig_s, own_r, near_r, far_r, wide_s, wide_r,
+    prod, gprod, zval, inv_b, fac_b, z_s, z_r, out_v, ggate_v, gsig_s, own_r, near_r, far_r, wide_s, wide_r,
     gf_s, gf_r, gz_s,
-    inside_sem, load_sem, za_s, za_r, zr_s, zr_r, zf_s, zf_r, ga_s, ga_r, ca_s, ca_r, yf_s, yf_r, xh_s, xh_r, n_ss, n_rs, w_ss, w_rs,
+    inside_sem, load_sem, store_sem, za_s, za_r, zr_s, zr_r, zf_s, zf_r, ga_s, ga_r, ca_s, ca_r, yf_s, yf_r, xh_s, xh_r, n_ss, n_rs, w_ss, w_rs,
     df_s, df_r, dh_s, dh_r, zb_s, zb_r, sb_s, sb_r, gx_ss, gx_rs, gz_ss, gz_rs,
 ):
     seq, tpi = lax.axis_index("seq"), lax.axis_index("tp")
@@ -121,7 +121,6 @@
                 source.at[lax.rem(z + k, Q)], result.at[:, lanes], ssem.at[k - 1], rsem.at[k - 1], at(x, z + k, y)
             )
             copies[k].start()
-        result[:, lanes] = source[z]
         return copies
 
     def transform(tbl, buf, start, count, result):
@@ -266,15 +265,18 @@
 
     lax.fori_loop(0, T // 8, forward_tile, 0)
     conv = inverse(slice(T, 2 * T), prod[...])
-    for copies in (g_copies, c_copies):
-        for k in (1, 3, 2):
-            copies[k].wait_recv()
 
     ones = jnp.ones((2 * C, C), BF16)
     lane = lax.broadcasted_iota(jnp.int32, (T, C), 1)
     sums = jnp.zeros((T, C), F32)
     for zp in range(Q):
-        mixed = conv[:, zp * C : (zp + 1) * C] + skip_v[...] * xbuf[8 + 4 * zp + y].astype(F32)
+        zval[zp] = conv[:, zp * C : (zp + 1) * C]
+    for k in (0, 1, 3, 2):
+        zp = lax.rem(z + Q - k, Q)
+        if k:
+            g_copies[k].wait_recv()
+            c_copies[k].wait_recv()
+        mixed = zval[zp] + skip_v[...] * xbuf[8 + 4 * zp + y].astype(F32)
         zval[zp] = mixed
         z_s[zp, 0] = mixed.astype(BF16)
         z_s[zp, 1] = (mixed - mixed.astype(BF16).astype(F32)).astype(BF16)
@@ -462,7 +464,6 @@
     gz_s[...] = total
     gz_copies = back_along_z(gz_s, gfilt, gz_ss, gz_rs)
     signal_gradient(z)
-    gsig[:, lanes] = gsig_s[z]
 
     z_r[z] = z_s[z]
     for copy in zb_copies:
@@ -473,13 +474,17 @@
         mixed = z_r[j, 0].astype(F32) + z_r[j, 1].astype(F32)
         gated = gate_v[:, cols].astype(F32) * mixed
         dgated = cot_v[:, cols].astype(F32) * inv - gated * fac
-        out[:, cols] = (gated * inv).astype(BF16)
-        ggate[:, cols] = (dgated * mixed).astype(BF16)
-
-    for copy in s_copies:
-        copy.wait()
-    for copy in gz_copies.values():
-        copy.wait()
+        out_v[:, cols] = (gated * inv).astype(BF16)
+        ggate_v[:, cols] = (dgated * mixed).astype(BF16)
+
+    stores = [
+        pltpu.make_async_copy(out_v, out, store_sem.at[0]),
+        pltpu.make_async_copy(ggate_v, ggate, store_sem.at[1]),
+        pltpu.make_async_copy(gsig_s.at[z], gsig.at[:, lanes], store_sem.at[2]),
+        pltpu.make_async_copy(gz_s.at[z], gfilt.at[:, lanes], store_sem.at[3]),
+    ]
+    for copy in stores:
+        copy.start()
     for copy in waits:
         copy.wait_send()
     for needed, copy in sent:
@@ -487,6 +492,10 @@
             copy.wait_send()
         else:
             pl.when(needed)(copy.wait_send)
+    for copy in s_copies:
+        copy.wait()
+    for copy in list(gz_copies.values()) + stores:
+        copy.wait()
 
 
 def finish(a, b, c, d, e, f, g, h, sems):
@@ -514,11 +523,11 @@
         pltpu.VMEM((LAGS, T, C), F32), pltpu.VMEM((LAGS, T, C), F32), pltpu.VMEM((LAGS, T, C), F32),
         pltpu.VMEM((2 * T, Q * C), F32), pltpu.VMEM((2 * T, LAGS * C), F32), pltpu.VMEM((Q, T, C), F32),
         pltpu.VMEM((Q, T, C), F32), pltpu.VMEM((Q, T, C), F32),
-        pltpu.VMEM((Q, 2, T, C), BF16), pltpu.VMEM((Q, 2, T, C), BF16), pltpu.VMEM((Q, T, C), BF16),
+        pltpu.VMEM((Q, 2, T, C), BF16), pltpu.VMEM((Q, 2, T, C), BF16), pltpu.VMEM(block, BF16), pltpu.VMEM(block, BF16), pltpu.VMEM((Q, T, C), BF16),
         pltpu.VMEM((8, T), F32), pltpu.VMEM((9, 8, T), F32), pltpu.VMEM((2, 8, T), F32),
         pltpu.VMEM((8, T), F32), pltpu.VMEM((2, 8, T), F32),
         pltpu.VMEM((Q, Q, 4, 16, C), BF16), pltpu.VMEM((15, 4, 16, C), BF16), pltpu.VMEM((4, 16, C), F32),
-        pltpu.SemaphoreType.REGULAR, dma(10), *three, dma(2), dma(2), dma(2), dma(2), *three, *three, dma(4, 3), dma(4, 3), dma(4, 4), dma(2, 4), dma(11), dma(11), dma(2), dma(2),
+        pltpu.SemaphoreType.REGULAR, dma(10), dma(4), *three, dma(2), dma(2), dma(2), dma(2), *three, *three, dma(4, 3), dma(4, 3), dma(4, 4), dma(2, 4), dma(11), dma(11), dma(2), dma(2),
         dma(4, 3), dma(4, 3), dma(2, 4), dma(2, 4), *three, *three, dma(15), dma(15), *three,
     ]
     shapes = (
@@ -529,7 +538,7 @@
         kernel,
         out_shape=shapes,
         in_specs=[hbm] * 7,
-        out_specs=(vmem,) * 4,
+        out_specs=(hbm,) * 4,
         scratch_shapes=scratch,
         compiler_params=pltpu.CompilerParams(
             collective_id=0, has_side_effects=True, vmem_limit_bytes=63 << 20

time: 72.8 us -> 72.2 us (level)
  the two profiles are of different devices: /device:TPU:8 before, /device:TPU:96 now
where the time goes in v4:
time: 72.2 us; the launch traced here: 72 us
  Pallas kernels  71.4 us (99%)
    pallas_call x1, Pallas kernels, on_device(): pl.pallas_call(kernel, out_shape=shapes, in_specs=[hbm] * 7, out_specs=(h...  69.5 us
    pallas_call x1, Pallas kernels, on_device(): pl.pallas_call(finish, out_shape=shapes, in_specs=[vmem] * 4, out_specs=(...  1.81 us

profile of v4, /device:TPU:96, one launch (start us, length us, event | category | flops | bytes accessed | tf_op | source)
XLA Modules:
  0.0 72.0 jit_solution(15441917809053051423)
XLA Ops:
  0.6 69.5 %hyena.1 = (bf16[128,512]{1,0:T(8,128)(2,1)}, bf16[128,512]{1,0:T(8,128)(2,1)}, bf16[128,512]{1,0:T(8,128)(2,1)}, f32[16,512]{1,0:T(8,128)}) custom-call(s32[16]{0:T(128)} %docs.1, f32[1,512]{1,0:T(1,128)} %bitcast.1, bf16[128,512]{1,0:T(8,128)(2,1)} %signal.1, bf16[128,512]{1,0:T(8,128)(2,1)} %gate.1, bf16[1024,512]{1,0:T(8,128)(2,1)} %filters.1, ...), custom_call_target="tpu_custom_call" | custom-call | tf_op jit(solution)/shard_map/hyena/pallas_call | solution.py:537
  70.2 1.8 %finish.1 = (bf16[128,512]{1,0:T(8,128)(2,1)}, bf16[128,512]{1,0:T(8,128)(2,1)}, bf16[128,512]{1,0:T(8,128)(2,1)}, f32[16,512]{1,0:T(8,128)}) custom-call(bf16[128,512]{1,0:T(8,128)(2,1)} %get-tuple-element.8.a, bf16[128,512]{1,0:T(8,128)(2,1)} %get-tuple-element.9.b, bf16[128,512]{1,0:T(8,128)(2,1)} %get-tuple-element.10.c, f32[16,512]{1,0:T(8,128)} %get-tuple-element.11.d), custom_call_target="tpu_custom_call" | custom-call | tf_op jit(solution)/shard_map/finish/pallas_call | solution.py:548

commit v5 on v4

--- a/solution.py
+++ b/solution.py
@@ -454,8 +454,6 @@
 
     arrive(quads[4])
     arrive(quads[5])
-    give(2)
-
     for copy in gx_copies:
         copy.wait_recv()
     total = gf_s[x, y].astype(F32)
@@ -463,6 +461,8 @@
         total += gf_r[n].astype(F32)
     gz_s[...] = total
     gz_copies = back_along_z(gz_s, gfilt, gz_ss, gz_rs)
+    give(2)
+
     signal_gradient(z)
 
     z_r[z] = z_s[z]

time: 72.2 us -> 72 us (level)
  no operation moved by 1% of the time
where the time goes in v5:
time: 72 us; the launch traced here: 71.9 us
  Pallas kernels  71.2 us (99%)
    pallas_call x1, Pallas kernels, on_device(): pl.pallas_call(kernel, out_shape=shapes, in_specs=[hbm] * 7, out_specs=(h...  69.4 us
    pallas_call x1, Pallas kernels, on_device(): pl.pallas_call(finish, out_shape=shapes, in_specs=[vmem] * 4, out_specs=(...  1.81 us

profile of v5, /device:TPU:96, one launch (start us, length us, event | category | flops | bytes accessed | tf_op | source)
XLA Modules:
  0.0 71.9 jit_solution(10416572799718865633)
XLA Ops:
  0.6 69.4 %hyena.1 = (bf16[128,512]{1,0:T(8,128)(2,1)}, bf16[128,512]{1,0:T(8,128)(2,1)}, bf16[128,512]{1,0:T(8,128)(2,1)}, f32[16,512]{1,0:T(8,128)}) custom-call(s32[16]{0:T(128)} %docs.1, f32[1,512]{1,0:T(1,128)} %bitcast.1, bf16[128,512]{1,0:T(8,128)(2,1)} %signal.1, bf16[128,512]{1,0:T(8,128)(2,1)} %gate.1, bf16[1024,512]{1,0:T(8,128)(2,1)} %filters.1, ...), custom_call_target="tpu_custom_call" | custom-call | tf_op jit(solution)/shard_map/hyena/pallas_call | solution.py:537
  70.0 1.8 %finish.1 = (bf16[128,512]{1,0:T(8,128)(2,1)}, bf16[128,512]{1,0:T(8,128)(2,1)}, bf16[128,512]{1,0:T(8,128)(2,1)}, f32[16,512]{1,0:T(8,128)}) custom-call(bf16[128,512]{1,0:T(8,128)(2,1)} %get-tuple-element.8.a, bf16[128,512]{1,0:T(8,128)(2,1)} %get-tuple-element.9.b, bf16[128,512]{1,0:T(8,128)(2,1)} %get-tuple-element.10.c, f32[16,512]{1,0:T(8,128)} %get-tuple-element.11.d), custom_call_target="tpu_custom_call" | custom-call | tf_op jit(solution)/shard_map/finish/pallas_call | solution.py:548
